TPU v7x, 32 devices: a whole 2x2x4 slice. The times are simulated.
32 devices in a mesh: row: 4 (over z), col: 4 (over x, core), fr: 2 (over y).
Axes of the slice: x: 2, y: 2, z: 4, core: 2. Of those that a mesh axis runs over, the one named last changes fastest.
Arguments:
- sigma_aa: float32 [3072, 12288], P(('fr', 'row'), 'col'), parts along dimension 0, may hold values from -6 to 6
- l_as: float32 [24576, 6144], P(('fr', 'row'), 'col'), parts along dimension 0, may hold values from -0.078125 to 0.078125
- block_mask: int32 [8, 4], P(('fr', 'row'), 'col'), parts along dimension 0, may hold values 0 or 1
Outputs:
- sigma_as: float32 [3072, 6144], P(('fr', 'row'), 'col'), parts along dimension 0
There are 2 independent parts, one for each index of `fr`. A program takes and returns all parts, laid end to end along the dimension named above; each array names one. Nothing has to cross between parts.
All inputs are finite; a program needn't handle non-finite values. No bound on the sum of `block_mask` on one device may be relied on, other than what follows from the above.
Results may differ from a plain program's by a relative error of at most 0.0003.
Values sent between devices are 32-bit elements; how exact they have to be, the bound alone decides.
No kernel may reach another device: no remote copies, remote signals or barrier semaphores. Data moves between devices by JAX's collectives and lax.ppermute only.
A program may use at most 128 MiB of HBM per device.

v0:
```python
import jax
import jax.numpy as jnp
from jax import lax
from jax.sharding import PartitionSpec as P


def shifted(block, rows_by, cols_by):
    rows, cols = lax.axis_size("row"), lax.axis_size("col")
    route = [
        (r * cols + c, (r + rows_by) % rows * cols + (c + cols_by) % cols) for r in range(rows) for c in range(cols)
    ]
    return lax.ppermute(block, ("row", "col"), route)


def product(lhs_block, rhs_block):
    return jnp.dot(lhs_block, rhs_block, preferred_element_type=jnp.float32, precision=lax.Precision.HIGH)


def body(sigma_aa, l_as, block_mask):
    half_steps = lax.axis_size("row") // 2
    sign = -block_mask[0, 0].astype(jnp.float32)
    chunks = 2
    size = sigma_aa.shape[0] // chunks
    outs = []
    for chunk in range(chunks):
        own = sigma_aa[chunk * size : (chunk + 1) * size]
        total = None
        for turn in reversed(range(half_steps)):
            visiting = shifted(own, turn, -turn) if turn else own
            term = sign * product(visiting, l_as)
            total = term if total is None else shifted(total, -1, 0) + term
        outs.append(total)
    return jnp.concatenate(outs, 0)


def solution(mesh):
    placed = (P(("fr", "row"), "col"), P(("fr", "row"), "col"), P(("fr", "row"), "col"))
    return jax.shard_map(
        body, mesh=mesh, in_specs=placed, out_specs=P(("fr", "row"), "col"), check_vma=False
    )
```

profile of v0, /device:TPU:3, one launch (start us, length us, event | category | flops | bytes accessed | tf_op | source)
XLA Modules:
  0.0 179.2 jit_solution(12632603971321922574)
XLA Ops:
  0.0 4.3 %fusion.2 = (f32[192,3072]{1,0:T(8,128)}, f32[192,3072]{1,0:T(8,128)S(1)}) fusion(f32[384,3072]{1,0:T(8,128)} %param.3), kind=kLoop, calls=%fused_computation.7 | loop fusion | bytes 9437184 | tf_op jit(solution)/shard_map/slice | solution.py:26
  4.3 1.9 %collective-permute-start.2 = (f32[192,3072]{1,0:T(8,128)S(1)}, f32[192,3072]{1,0:T(8,128)S(1)}, u32[]{:S(2)}, u32[]{:S(2)}) collective-permute-start(f32[192,3072]{1,0:T(8,128)S(1)} %get-tuple-element.6), channel_id=1, source_target_pairs={{0,14},{2,8},{4,10},{6,12},{8,22},{10,16},{12,18},{14,20},{16,30},... | collective-permute-start | bytes 7077896 | tf_op jit(solution)/shard_map/ppermute | solution.py:12
  6.2 1.0 collective-permute-start
  7.8 52.8 %collective-permute-done.2 = f32[192,3072]{1,0:T(8,128)S(1)} collective-permute-done((f32[192,3072]{1,0:T(8,128)S(1)}, f32[192,3072]{1,0:T(8,128)S(1)}, u32[]{:S(2)}, u32[]{:S(2)}) %collective-permute-start.2) | collective-permute-done | bytes 2359328 | tf_op jit(solution)/shard_map/ppermute | solution.py:12
  60.6 0.0 copy-start.1
  60.6 1.4 copy-done.1
  62.0 0.0 copy-start
  62.0 11.6 %convolution_multiply_fusion.1 = f32[192,1536]{1,0:T(8,128)S(1)} fusion(f32[192,3072]{1,0:T(8,128)} %copy-done.1, f32[3072,1536]{1,0:T(8,128)} %param.4, f32[]{:T(128)} %bitcast), kind=kOutput, calls=%fused_computation.1 | convolution fusion | flops 5436112896 | bytes 22413316 | tf_op jit(solution)/shard_map/dot_general | solution.py:16
  73.6 1.5 collective-permute-start.3
  75.1 36.1 %collective-permute-done = f32[192,3072]{1,0:T(8,128)S(1)} collective-permute-done((f32[192,3072]{1,0:T(8,128)}, f32[192,3072]{1,0:T(8,128)S(1)}, u32[]{:S(2)}, u32[]{:S(2)}) %collective-permute-start) | collective-permute-done | bytes 2359328 | tf_op jit(solution)/shard_map/ppermute | solution.py:12
  111.2 0.0 copy-done
  111.2 8.0 %convolution_multiply_fusion.3 = f32[192,1536]{1,0:T(8,128)} fusion(f32[192,3072]{1,0:T(8,128)S(1)} %collective-permute-done, f32[3072,1536]{1,0:T(8,128)S(1)} %copy-done, f32[]{:T(128)} %bitcast), kind=kOutput, calls=%fused_computation.3 | convolution fusion | flops 5436112896 | bytes 22413316 | tf_op jit(solution)/shard_map/dot_general | solution.py:16
  119.2 38.4 %collective-permute-start.1 = (f32[192,1536]{1,0:T(8,128)}, f32[192,1536]{1,0:T(8,128)}, u32[]{:S(2)}, u32[]{:S(2)}) collective-permute-start(f32[192,1536]{1,0:T(8,128)} %convolution_multiply_fusion.3), channel_id=1, source_target_pairs={{0,24},{2,26},{4,28},{6,30},{8,0},{10,2},{12,4},{14,6},{16,8},{18,... | collective-permute-start | bytes 3538952 | tf_op jit(solution)/shard_map/ppermute | solution.py:12
  157.6 8.6 %convolution_multiply_fusion = f32[192,1536]{1,0:T(8,128)S(1)} fusion(f32[3072,1536]{1,0:T(8,128)S(1)} %copy-done, f32[]{:T(128)} %bitcast, f32[384,3072]{1,0:T(8,128)} %param.3), kind=kOutput, calls=%fused_computation | convolution fusion | flops 5436112896 | bytes 22413824 | tf_op jit(solution)/shard_map/dot_general | solution.py:16
  166.2 8.6 %convolution_multiply_fusion.2 = f32[192,1536]{1,0:T(8,128)S(1)} fusion(f32[3072,1536]{1,0:T(8,128)S(1)} %copy-done, f32[]{:T(128)} %bitcast, f32[384,3072]{1,0:T(8,128)} %param.3), kind=kOutput, calls=%fused_computation.2 | convolution fusion | flops 5436112896 | bytes 22413824 | tf_op jit(solution)/shard_map/dot_general | solution.py:16
  174.8 0.0 collective-permute-done.3
  174.8 1.4 add.7
  176.2 0.0 collective-permute-done.1
  176.2 1.4 add.6
  177.6 1.6 pad_maximum_fusion
Async XLA Ops:
  4.3 56.3 %collective-permute-start.2 = (f32[192,3072]{1,0:T(8,128)S(1)}, f32[192,3072]{1,0:T(8,128)S(1)}, u32[]{:S(2)}, u32[]{:S(2)}) collective-permute-start(f32[192,3072]{1,0:T(8,128)S(1)} %get-tuple-element.6), channel_id=1, source_target_pairs={{0,14},{2,8},{4,10},{6,12},{8,22},{10,16},{12,18},{14,20},{16,30},... | collective-permute-start | bytes 7077896 | tf_op jit(solution)/shard_map/ppermute | solution.py:12
  6.2 105.0 %collective-permute-start = (f32[192,3072]{1,0:T(8,128)}, f32[192,3072]{1,0:T(8,128)S(1)}, u32[]{:S(2)}, u32[]{:S(2)}) collective-permute-start(f32[192,3072]{1,0:T(8,128)} %get-tuple-element.5), channel_id=1, source_target_pairs={{0,14},{2,8},{4,10},{6,12},{8,22},{10,16},{12,18},{14,20},{16,30},... | collective-permute-start | bytes 7077896 | tf_op jit(solution)/shard_map/ppermute | solution.py:12
  60.6 1.4 copy-start.1
  62.0 49.2 %copy-start = (f32[3072,1536]{1,0:T(8,128)S(1)}, f32[3072,1536]{1,0:T(8,128)}, u32[]{:S(2)}) copy-start(f32[3072,1536]{1,0:T(8,128)} %param.4) | copy-start | bytes 56623108
  73.6 101.2 %collective-permute-start.3 = (f32[192,1536]{1,0:T(8,128)S(1)}, f32[192,1536]{1,0:T(8,128)}, u32[]{:S(2)}, u32[]{:S(2)}) collective-permute-start(f32[192,1536]{1,0:T(8,128)S(1)} %convolution_multiply_fusion.1), channel_id=1, source_target_pairs={{0,24},{2,26},{4,28},{6,30},{8,0},{10,2},{12,4},{14,6},{16,8},{18,... | collective-permute-start | bytes 3538952 | tf_op jit(solution)/shard_map/ppermute | solution.py:12
  119.2 57.0 %collective-permute-start.1 = (f32[192,1536]{1,0:T(8,128)}, f32[192,1536]{1,0:T(8,128)}, u32[]{:S(2)}, u32[]{:S(2)}) collective-permute-start(f32[192,1536]{1,0:T(8,128)} %convolution_multiply_fusion.3), channel_id=1, source_target_pairs={{0,24},{2,26},{4,28},{6,30},{8,0},{10,2},{12,4},{14,6},{16,8},{18,... | collective-permute-start | bytes 3538952 | tf_op jit(solution)/shard_map/ppermute | solution.py:12
where the time goes:
time: 179 us
  waiting for transfers between devices  88.9 us (50%)
  starting transfers between devices  42.7 us (24%)
  matrix products  36.7 us (21%)
  local copies, waits for them, and re-layouts  5.72 us (3%)
  other arithmetic  4.37 us (2%)
    ppermute x4, waiting for transfers between devices, shifted(): return lax.ppermute(block, ('row', 'col'), route)  88.9 us
    ppermute x4, starting transfers between devices, shifted(): return lax.ppermute(block, ('row', 'col'), route)  42.7 us
    dot_general x4, matrix products, product(): jnp.dot(lhs_block, rhs_block, preferred_element_type=jnp.float32, precisi...  36.7 us
    slice x1, local copies, waits for them, and re-layouts, body(): own = sigma_aa[chunk * size:(chunk + 1) * size]  4.31 us
  transfers between devices with their start and end apart: 4, of which 2 were waited for; matrix products, arithmetic and copies ran while one was open for 21% of the time, Pallas kernels for 0%

commit v1 on v0

--- a/solution.py
+++ b/solution.py
@@ -2,6 +2,10 @@
 import jax.numpy as jnp
 from jax import lax
 from jax.sharding import PartitionSpec as P
+
+
+CUTS = (0, 4, 24, 40, 48)
+HOLD = {0: 2, 1: 3, 2: 3}
 
 
 def shifted(block, rows_by, cols_by):
@@ -18,19 +22,26 @@
 
 def body(sigma_aa, l_as, block_mask):
     half_steps = lax.axis_size("row") // 2
+    rows = sigma_aa.shape[0]
     sign = -block_mask[0, 0].astype(jnp.float32)
-    chunks = 2
-    size = sigma_aa.shape[0] // chunks
+    cuts = [rows * cut // CUTS[-1] for cut in CUTS]
+    pieces = [sigma_aa[a:b] for a, b in zip(cuts, cuts[1:])]
+    visits = [[shifted(piece, turn, -turn) for turn in range(1, half_steps)] for piece in pieces]
+    own = sign * product(sigma_aa, l_as)
+    own, visits[0] = lax.optimization_barrier((own, visits[0]))
     outs = []
-    for chunk in range(chunks):
-        own = sigma_aa[chunk * size : (chunk + 1) * size]
-        total = None
-        for turn in reversed(range(half_steps)):
-            visiting = shifted(own, turn, -turn) if turn else own
-            term = sign * product(visiting, l_as)
-            total = term if total is None else shifted(total, -1, 0) + term
-        outs.append(total)
-    return jnp.concatenate(outs, 0)
+    for index, visit in enumerate(visits):
+        total = sign * product(visit[-1], l_as)
+        later = HOLD.get(index)
+        if index + 1 < len(visits):
+            anchor, visits[index + 1][-1] = lax.optimization_barrier((total, visits[index + 1][-1]))
+        if later is not None:
+            total, visits[later][-1] = lax.optimization_barrier((total, visits[later][-1]))
+        for visiting in reversed(visit[:-1]):
+            total = shifted(total, -1, 0) + sign * product(visiting, l_as)
+        outs.append(shifted(total, -1, 0))
+    early = jnp.concatenate([*outs[:-1], jnp.zeros_like(outs[-1])], 0) + own
+    return lax.dynamic_update_slice(early, outs[-1] + own[cuts[-2] :], (cuts[-2], 0))
 
 
 def solution(mesh):

time: 179 us -> 161 us (0.90); the launches traced: 179 us -> 159 us
  starting transfers between devices: 42.7 us -> 11.9 us
  matrix products: 36.7 us -> 53.4 us
  waiting for transfers between devices: 88.9 us -> 86.3 us
  other arithmetic: 4.37 us -> 2.52 us
    ppermute x4 -> x8, starting transfers between devices: 42.7 us -> 11.9 us  [shifted(): return lax.ppermute(block, ('row', 'col'), route)]
    dot_general x4 -> x5, matrix products: 36.7 us -> 53.4 us  [product(): jnp.dot(lhs_block, rhs_block, preferred_element_type=jnp.float32, precisi...]
    ppermute x4 -> x8, waiting for transfers between devices: 88.9 us -> 86.3 us  [shifted(): return lax.ppermute(block, ('row', 'col'), route)]
    slice x1 -> x4, local copies, waits for them, and re-layouts: 4.31 us -> 4.41 us  [body(): pieces = [sigma_aa[a:b] for a, b in zip(cuts, cuts[1:])]]
  transfers between devices with their start and end apart: 4 -> 8, of which waited for: 2 -> 4; matrix products, arithmetic and copies ran while one was open for 21% -> 37% of each run, Pallas kernels for 0% -> 0%
where the time goes in v1:
time: 161 us; the launch traced here: 159 us
  waiting for transfers between devices  86.3 us (54%)
  matrix products  53.4 us (33%)
  starting transfers between devices  11.9 us (7%)
  local copies, waits for them, and re-layouts  4.5 us (3%)
  other arithmetic  2.52 us (2%)
    ppermute x8, waiting for transfers between devices, shifted(): return lax.ppermute(block, ('row', 'col'), route)  86.3 us
    dot_general x5, matrix products, product(): jnp.dot(lhs_block, rhs_block, preferred_element_type=jnp.float32, precisi...  53.4 us
    ppermute x8, starting transfers between devices, shifted(): return lax.ppermute(block, ('row', 'col'), route)  11.9 us
    slice x4, local copies, waits for them, and re-layouts, body(): pieces = [sigma_aa[a:b] for a, b in zip(cuts, cuts[1:])]  4.41 us
  transfers between devices with their start and end apart: 8, of which 4 were waited for; matrix products, arithmetic and copies ran while one was open for 37% of the time, Pallas kernels for 0%

profile of v1, /device:TPU:3, one launch (start us, length us, event | category | flops | bytes accessed | tf_op | source)
XLA Modules:
  0.0 159.4 jit_solution(4881503717435694824)
XLA Ops:
  0.0 1.0 slice.15
  1.0 1.9 %collective-permute-start = (f32[32,3072]{1,0:T(8,128)S(1)}, f32[32,3072]{1,0:T(8,128)S(1)}, u32[]{:S(2)}, u32[]{:S(2)}) collective-permute-start(f32[32,3072]{1,0:T(8,128)S(1)} %slice.15), channel_id=1, source_target_pairs={{0,14},{2,8},{4,10},{6,12},{8,22},{10,16},{12,18},{14,20},{16,30},... | collective-permute-start | bytes 1179656 | tf_op jit(solution)/shard_map/ppermute | solution.py:16
  2.9 1.8 %slice.17 = f32[160,3072]{1,0:T(8,128)S(1)} slice(f32[384,3072]{1,0:T(8,128)} %param.3), slice={[32:192], [0:3072]} | slice | bytes 3932160 | tf_op jit(solution)/shard_map/slice | solution.py:28
  4.8 1.0 collective-permute-start.3
  5.8 1.5 slice.16
  7.3 1.9 %collective-permute-start.1 = (f32[128,3072]{1,0:T(8,128)S(1)}, f32[128,3072]{1,0:T(8,128)S(1)}, u32[]{:S(2)}, u32[]{:S(2)}) collective-permute-start(f32[128,3072]{1,0:T(8,128)S(1)} %slice.16), channel_id=1, source_target_pairs={{0,14},{2,8},{4,10},{6,12},{8,22},{10,16},{12,18},{14,20},{16,30},... | collective-permute-start | bytes 4718600 | tf_op jit(solution)/shard_map/ppermute | solution.py:16
  9.2 0.1 slice.18
  9.3 0.6 collective-permute-start.4
  10.6 15.3 %convolution_multiply_fusion = f32[384,1536]{1,0:T(8,128)S(1)} fusion(f32[384,3072]{1,0:T(8,128)S(1)} %copy-done, f32[3072,1536]{1,0:T(8,128)} %param.4, f32[]{:T(128)} %bitcast), kind=kOutput, calls=%fused_computation | convolution fusion | flops 10872225792 | bytes 25952260 | tf_op jit(solution)/shard_map/dot_general | solution.py:20
  25.9 0.1 pad.3.clone
  26.0 9.3 %convolution_multiply_fusion.4 = f32[32,1536]{1,0:T(8,128)S(1)} fusion(f32[32,3072]{1,0:T(8,128)S(1)} %collective-permute-done, f32[3072,1536]{1,0:T(8,128)} %param.4, f32[]{:T(128)} %bitcast), kind=kOutput, calls=%fused_computation.5 | convolution fusion | flops 906018816 | bytes 19464196 | tf_op jit(solution)/shard_map/dot_general | solution.py:20
  35.3 55.8 %collective-permute-done.1 = f32[128,3072]{1,0:T(8,128)S(1)} collective-permute-done((f32[128,3072]{1,0:T(8,128)S(1)}, f32[128,3072]{1,0:T(8,128)S(1)}, u32[]{:S(2)}, u32[]{:S(2)}) %collective-permute-start.1) | collective-permute-done | bytes 1572896 | tf_op jit(solution)/shard_map/ppermute | solution.py:16
  91.1 1.4 collective-permute-start.2
  92.5 9.8 %convolution_multiply_fusion.1 = f32[160,1536]{1,0:T(8,128)S(1)} fusion(f32[160,3072]{1,0:T(8,128)S(1)} %collective-permute-done.3, f32[3072,1536]{1,0:T(8,128)} %param.4, f32[]{:T(128)} %bitcast), kind=kOutput, calls=%fused_computation.1 | convolution fusion | flops 4530094080 | bytes 21823492 | tf_op jit(solution)/shard_map/dot_general | solution.py:20
  102.4 5.6 %collective-permute-done.4 = f32[64,3072]{1,0:T(8,128)S(1)} collective-permute-done((f32[64,3072]{1,0:T(8,128)S(1)}, f32[64,3072]{1,0:T(8,128)S(1)}, u32[]{:S(2)}, u32[]{:S(2)}) %collective-permute-start.4) | collective-permute-done | bytes 786464 | tf_op jit(solution)/shard_map/ppermute | solution.py:16
  108.0 4.8 %collective-permute-start.5 = (f32[160,1536]{1,0:T(8,128)S(1)}, f32[160,1536]{1,0:T(8,128)S(1)}, u32[]{:S(2)}, u32[]{:S(2)}) collective-permute-start(f32[160,1536]{1,0:T(8,128)S(1)} %convolution_multiply_fusion.1), channel_id=1, source_target_pairs={{0,24},{2,26},{4,28},{6,30},{8,0},{10,2},{12,4},{14,6},{16,8},{18,... | collective-permute-start | bytes 2949128 | tf_op jit(solution)/shard_map/ppermute | solution.py:16
  112.8 9.2 %convolution_multiply_fusion.2 = f32[128,1536]{1,0:T(8,128)S(1)} fusion(f32[128,3072]{1,0:T(8,128)S(1)} %collective-permute-done.1, f32[3072,1536]{1,0:T(8,128)} %param.4, f32[]{:T(128)} %bitcast), kind=kOutput, calls=%fused_computation.2 | convolution fusion | flops 3624075264 | bytes 21233668 | tf_op jit(solution)/shard_map/dot_general | solution.py:20
  122.0 0.1 collective-permute-start.6
  122.1 9.8 %convolution_multiply_fusion.3 = f32[64,1536]{1,0:T(8,128)S(1)} fusion(f32[64,3072]{1,0:T(8,128)S(1)} %collective-permute-done.4, f32[3072,1536]{1,0:T(8,128)} %param.4, f32[]{:T(128)} %bitcast), kind=kOutput, calls=%fused_computation.4 | convolution fusion | flops 1812037632 | bytes 20054020 | tf_op jit(solution)/shard_map/dot_general | solution.py:20
  131.9 0.1 collective-permute-start.7
  132.0 18.2 %collective-permute-done.6 = f32[128,1536]{1,0:T(8,128)S(1)} collective-permute-done((f32[128,1536]{1,0:T(8,128)S(1)}, f32[128,1536]{1,0:T(8,128)S(1)}, u32[]{:S(2)}, u32[]{:S(2)}) %collective-permute-start.6) | collective-permute-done | bytes 786464 | tf_op jit(solution)/shard_map/ppermute | solution.py:16
  150.2 1.7 %maximum_add_fusion = f32[384,1536]{1,0:T(8,128)} fusion(f32[384,1536]{1,0:T(8,128)S(1)} %convolution_multiply_fusion, f32[128,1536]{1,0:T(8,128)S(1)} %collective-permute-done.6, f32[160,1536]{1,0:T(8,128)S(1)} %collective-permute-done.5, f32[32,1536]{1,0:T(8,128)S(1)} %collective-permute-done.2, f32[384]{0:T(512)S(1)} %pad.3.clone), kind=kLoop, calls=%fused_computation.3 | loop fusion | flops 2359296 | bytes 6686208 | tf_op jit(solution)/shard_map/add | solution.py:43
  151.9 6.7 %collective-permute-done.7 = f32[64,1536]{1,0:T(8,128)S(1)} collective-permute-done((f32[64,1536]{1,0:T(8,128)S(1)}, f32[64,1536]{1,0:T(8,128)S(1)}, u32[]{:S(2)}, u32[]{:S(2)}) %collective-permute-start.7) | collective-permute-done | bytes 393248 | tf_op jit(solution)/shard_map/ppermute | solution.py:16
  158.6 0.8 add_dynamic-update-slice_fusion
  (7 shorter events, 0.0 us)
Async XLA Ops:
  1.0 25.0 %collective-permute-start = (f32[32,3072]{1,0:T(8,128)S(1)}, f32[32,3072]{1,0:T(8,128)S(1)}, u32[]{:S(2)}, u32[]{:S(2)}) collective-permute-start(f32[32,3072]{1,0:T(8,128)S(1)} %slice.15), channel_id=1, source_target_pairs={{0,14},{2,8},{4,10},{6,12},{8,22},{10,16},{12,18},{14,20},{16,30},... | collective-permute-start | bytes 1179656 | tf_op jit(solution)/shard_map/ppermute | solution.py:16
  2.9 6.3 %copy-start = (f32[384,3072]{1,0:T(8,128)S(1)}, f32[384,3072]{1,0:T(8,128)}, u32[]{:S(2)}) copy-start(f32[384,3072]{1,0:T(8,128)} %param.3) | copy-start | bytes 14155780
  4.8 87.8 %collective-permute-start.3 = (f32[160,3072]{1,0:T(8,128)S(1)}, f32[160,3072]{1,0:T(8,128)S(1)}, u32[]{:S(2)}, u32[]{:S(2)}) collective-permute-start(f32[160,3072]{1,0:T(8,128)S(1)} %slice.17), channel_id=1, source_target_pairs={{0,14},{2,8},{4,10},{6,12},{8,22},{10,16},{12,18},{14,20},{16,30},... | collective-permute-start | bytes 5898248 | tf_op jit(solution)/shard_map/ppermute | solution.py:16
  7.3 83.8 %collective-permute-start.1 = (f32[128,3072]{1,0:T(8,128)S(1)}, f32[128,3072]{1,0:T(8,128)S(1)}, u32[]{:S(2)}, u32[]{:S(2)}) collective-permute-start(f32[128,3072]{1,0:T(8,128)S(1)} %slice.16), channel_id=1, source_target_pairs={{0,14},{2,8},{4,10},{6,12},{8,22},{10,16},{12,18},{14,20},{16,30},... | collective-permute-start | bytes 4718600 | tf_op jit(solution)/shard_map/ppermute | solution.py:16
  9.3 98.7 %collective-permute-start.4 = (f32[64,3072]{1,0:T(8,128)S(1)}, f32[64,3072]{1,0:T(8,128)S(1)}, u32[]{:S(2)}, u32[]{:S(2)}) collective-permute-start(f32[64,3072]{1,0:T(8,128)S(1)} %slice.18), channel_id=1, source_target_pairs={{0,14},{2,8},{4,10},{6,12},{8,22},{10,16},{12,18},{14,20},{16,30},... | collective-permute-start | bytes 2359304 | tf_op jit(solution)/shard_map/ppermute | solution.py:16
  91.1 40.9 %collective-permute-start.2 = (f32[32,1536]{1,0:T(8,128)S(1)}, f32[32,1536]{1,0:T(8,128)S(1)}, u32[]{:S(2)}, u32[]{:S(2)}) collective-permute-start(f32[32,1536]{1,0:T(8,128)S(1)} %convolution_multiply_fusion.4), channel_id=1, source_target_pairs={{0,24},{2,26},{4,28},{6,30},{8,0},{10,2},{12,4},{14,6},{16,8},{18,... | collective-permute-start | bytes 589832 | tf_op jit(solution)/shard_map/ppermute | solution.py:16
  108.0 42.2 %collective-permute-start.5 = (f32[160,1536]{1,0:T(8,128)S(1)}, f32[160,1536]{1,0:T(8,128)S(1)}, u32[]{:S(2)}, u32[]{:S(2)}) collective-permute-start(f32[160,1536]{1,0:T(8,128)S(1)} %convolution_multiply_fusion.1), channel_id=1, source_target_pairs={{0,24},{2,26},{4,28},{6,30},{8,0},{10,2},{12,4},{14,6},{16,8},{18,... | collective-permute-start | bytes 2949128 | tf_op jit(solution)/shard_map/ppermute | solution.py:16
  122.0 28.1 %collective-permute-start.6 = (f32[128,1536]{1,0:T(8,128)S(1)}, f32[128,1536]{1,0:T(8,128)S(1)}, u32[]{:S(2)}, u32[]{:S(2)}) collective-permute-start(f32[128,1536]{1,0:T(8,128)S(1)} %convolution_multiply_fusion.2), channel_id=1, source_target_pairs={{0,24},{2,26},{4,28},{6,30},{8,0},{10,2},{12,4},{14,6},{16,8},{18,... | collective-permute-start | bytes 2359304 | tf_op jit(solution)/shard_map/ppermute | solution.py:16
  131.9 26.7 %collective-permute-start.7 = (f32[64,1536]{1,0:T(8,128)S(1)}, f32[64,1536]{1,0:T(8,128)S(1)}, u32[]{:S(2)}, u32[]{:S(2)}) collective-permute-start(f32[64,1536]{1,0:T(8,128)S(1)} %convolution_multiply_fusion.3), channel_id=1, source_target_pairs={{0,24},{2,26},{4,28},{6,30},{8,0},{10,2},{12,4},{14,6},{16,8},{18,... | collective-permute-start | bytes 1179656 | tf_op jit(solution)/shard_map/ppermute | solution.py:16

commit v2 on v0

v2 whole, which is shorter than its diff:
```python
import jax
import jax.numpy as jnp
from jax import lax
from jax.sharding import PartitionSpec as P


CUTS = (0, 4, 26, 46, 48)


def shifted(block, rows_by, cols_by):
    rows, cols = lax.axis_size("row"), lax.axis_size("col")
    route = [
        (r * cols + c, (r + rows_by) % rows * cols + (c + cols_by) % cols) for r in range(rows) for c in range(cols)
    ]
    return lax.ppermute(block, ("row", "col"), route)


def after(value, *others):
    return lax.optimization_barrier((value, *others))[0]


def product(lhs_block, rhs_block):
    return jnp.dot(lhs_block, rhs_block, preferred_element_type=jnp.float32, precision=lax.Precision.HIGH)


def body(sigma_aa, l_as, block_mask):
    half_steps = lax.axis_size("row") // 2
    rows = sigma_aa.shape[0]
    sign = -block_mask[0, 0].astype(jnp.float32)
    cuts = [rows * cut // CUTS[-1] for cut in CUTS]
    pieces, block = [], sigma_aa
    for start, end in zip(cuts, cuts[1:]):
        piece, block = lax.optimization_barrier((block[start:end], block))
        pieces.append(piece)
    visits = [[shifted(piece, turn, -turn) for turn in range(1, half_steps)] for piece in pieces]
    first, second, third, last = [visit[-1] for visit in visits]

    def times_factor(block):
        return sign * product(block, l_as)

    def travel_back(total, piece):
        for visiting in reversed(visits[piece][:-1]):
            total = shifted(total, -1, 0) + times_factor(visiting)
        return shifted(total, -1, 0)

    own = times_factor(sigma_aa)
    first_total = times_factor(after(first, own))
    second_total = times_factor(after(second, first_total))
    first_out = travel_back(after(first_total, second_total, third), 0)
    second_out = travel_back(after(second_total, last), 1)
    third_total = times_factor(after(third, last, first_out))
    third_out = travel_back(third_total, 2)
    last_out = travel_back(times_factor(after(last, third_total)), 3)

    early = jnp.concatenate([first_out, second_out, third_out, jnp.zeros_like(last_out)], 0) + own
    return lax.dynamic_update_slice(early, last_out + own[cuts[3] :], (cuts[3], 0))


def solution(mesh):
    placed = (P(("fr", "row"), "col"), P(("fr", "row"), "col"), P(("fr", "row"), "col"))
    return jax.shard_map(
        body, mesh=mesh, in_specs=placed, out_specs=P(("fr", "row"), "col"), check_vma=False
    )
```

time: 179 us -> 159 us (0.89)
  starting transfers between devices: 42.7 us -> 10.9 us
  matrix products: 36.7 us -> 53.5 us
  local copies, waits for them, and re-layouts: 5.72 us -> 3.15 us
  other arithmetic: 4.37 us -> 2.38 us
    ppermute x4 -> x8, starting transfers between devices: 42.7 us -> 10.9 us  [shifted(): return lax.ppermute(block, ('row', 'col'), route)]
    dot_general x4 -> x5, matrix products: 36.7 us -> 53.5 us  [product(): jnp.dot(lhs_block, rhs_block, preferred_element_type=jnp.float32, precisi...]
    slice x1 -> x4, local copies, waits for them, and re-layouts: 4.31 us -> 3.07 us  [body(): piece, block = lax.optimization_barrier((block[start:end], block))]
    ppermute x4 -> x8, waiting for transfers between devices: 88.9 us -> 87.9 us  [shifted(): return lax.ppermute(block, ('row', 'col'), route)]
  transfers between devices with their start and end apart: 4 -> 8, of which waited for: 2 -> 7; matrix products, arithmetic and copies ran while one was open for 21% -> 36% of each run, Pallas kernels for 0% -> 0%
where the time goes in v2:
time: 159 us
  waiting for transfers between devices  87.9 us (55%)
  matrix products  53.5 us (34%)
  starting transfers between devices  10.9 us (7%)
  local copies, waits for them, and re-layouts  3.15 us (2%)
  other arithmetic  2.38 us (1%)
    ppermute x8, waiting for transfers between devices, shifted(): return lax.ppermute(block, ('row', 'col'), route)  87.9 us
    dot_general x5, matrix products, product(): jnp.dot(lhs_block, rhs_block, preferred_element_type=jnp.float32, precisi...  53.5 us
    ppermute x8, starting transfers between devices, shifted(): return lax.ppermute(block, ('row', 'col'), route)  10.9 us
  transfers between devices with their start and end apart: 8, of which 7 were waited for; matrix products, arithmetic and copies ran while one was open for 36% of the time, Pallas kernels for 0%

profile of v2, /device:TPU:3, one launch (start us, length us, event | category | flops | bytes accessed | tf_op | source)
XLA Modules:
  0.0 158.6 jit_solution(6552296479526209894)
XLA Ops:
  0.0 1.2 slice.15
  1.2 1.9 %collective-permute-start = (f32[32,3072]{1,0:T(8,128)S(1)}, f32[32,3072]{1,0:T(8,128)S(1)}, u32[]{:S(2)}, u32[]{:S(2)}) collective-permute-start(f32[32,3072]{1,0:T(8,128)S(1)} %slice.15), channel_id=1, source_target_pairs={{0,14},{2,8},{4,10},{6,12},{8,22},{10,16},{12,18},{14,20},{16,30},... | collective-permute-start | bytes 1179656 | tf_op jit(solution)/shard_map/ppermute | solution.py:15
  3.1 1.8 %slice.16 = f32[176,3072]{1,0:T(8,128)S(1)} slice(f32[384,3072]{1,0:T(8,128)} %param.3), slice={[32:208], [0:3072]} | slice | bytes 4325376 | tf_op jit(solution)/shard_map/slice | solution.py:33
  4.9 1.0 collective-permute-start.1
  5.9 0.1 slice.17
  6.0 1.9 %collective-permute-start.2 = (f32[160,3072]{1,0:T(8,128)S(1)}, f32[160,3072]{1,0:T(8,128)S(1)}, u32[]{:S(2)}, u32[]{:S(2)}) collective-permute-start(f32[160,3072]{1,0:T(8,128)S(1)} %slice.17), channel_id=1, source_target_pairs={{0,14},{2,8},{4,10},{6,12},{8,22},{10,16},{12,18},{14,20},{16,30},... | collective-permute-start | bytes 5898248 | tf_op jit(solution)/shard_map/ppermute | solution.py:15
  8.0 0.6 collective-permute-start.4
  9.2 15.3 %convolution_multiply_fusion = f32[384,1536]{1,0:T(8,128)S(1)} fusion(f32[384,3072]{1,0:T(8,128)S(1)} %copy-done, f32[3072,1536]{1,0:T(8,128)} %param.4, f32[]{:T(128)} %bitcast), kind=kOutput, calls=%fused_computation | convolution fusion | flops 10872225792 | bytes 25952260 | tf_op jit(solution)/shard_map/dot_general | solution.py:23
  24.6 9.3 %convolution_multiply_fusion.3 = f32[32,1536]{1,0:T(8,128)S(1)} fusion(f32[32,3072]{1,0:T(8,128)S(1)} %collective-permute-done, f32[3072,1536]{1,0:T(8,128)} %param.4, f32[]{:T(128)} %bitcast), kind=kOutput, calls=%fused_computation.4 | convolution fusion | flops 906018816 | bytes 19464196 | tf_op jit(solution)/shard_map/dot_general | solution.py:23
  33.9 27.9 %collective-permute-done.1 = f32[176,3072]{1,0:T(8,128)S(1)} collective-permute-done((f32[176,3072]{1,0:T(8,128)S(1)}, f32[176,3072]{1,0:T(8,128)S(1)}, u32[]{:S(2)}, u32[]{:S(2)}) %collective-permute-start.1) | collective-permute-done | bytes 2162720 | tf_op jit(solution)/shard_map/ppermute | solution.py:15
  61.7 10.4 %convolution_multiply_fusion.1 = f32[176,1536]{1,0:T(8,128)S(1)} fusion(f32[176,3072]{1,0:T(8,128)S(1)} %collective-permute-done.1, f32[3072,1536]{1,0:T(8,128)} %param.4, f32[]{:T(128)} %bitcast), kind=kOutput, calls=%fused_computation.1 | convolution fusion | flops 4983103488 | bytes 22118404 | tf_op jit(solution)/shard_map/dot_general | solution.py:23
  72.1 31.8 %collective-permute-done.2 = f32[160,3072]{1,0:T(8,128)S(1)} collective-permute-done((f32[160,3072]{1,0:T(8,128)S(1)}, f32[160,3072]{1,0:T(8,128)S(1)}, u32[]{:S(2)}, u32[]{:S(2)}) %collective-permute-start.2) | collective-permute-done | bytes 1966112 | tf_op jit(solution)/shard_map/ppermute | solution.py:15
  103.9 1.4 collective-permute-start.3
  105.3 1.4 collective-permute-done.4
  106.8 1.9 %collective-permute-start.5 = (f32[176,1536]{1,0:T(8,128)S(1)}, f32[176,1536]{1,0:T(8,128)S(1)}, u32[]{:S(2)}, u32[]{:S(2)}) collective-permute-start(f32[176,1536]{1,0:T(8,128)S(1)} %convolution_multiply_fusion.1), channel_id=1, source_target_pairs={{0,24},{2,26},{4,28},{6,30},{8,0},{10,2},{12,4},{14,6},{16,8},{18,... | collective-permute-start | bytes 3244040 | tf_op jit(solution)/shard_map/ppermute | solution.py:15
  108.6 3.2 %collective-permute-done.3 = f32[32,1536]{1,0:T(8,128)S(1)} collective-permute-done((f32[32,1536]{1,0:T(8,128)S(1)}, f32[32,1536]{1,0:T(8,128)S(1)}, u32[]{:S(2)}, u32[]{:S(2)}) %collective-permute-start.3) | collective-permute-done | bytes 196640 | tf_op jit(solution)/shard_map/ppermute | solution.py:15
  111.8 9.8 %convolution_multiply_fusion.2 = f32[160,1536]{1,0:T(8,128)S(1)} fusion(f32[160,3072]{1,0:T(8,128)S(1)} %collective-permute-done.2, f32[3072,1536]{1,0:T(8,128)} %param.4, f32[]{:T(128)} %bitcast), kind=kOutput, calls=%fused_computation.2 | convolution fusion | flops 4530094080 | bytes 21823492 | tf_op jit(solution)/shard_map/dot_general | solution.py:23
  121.6 2.1 %collective-permute-start.6 = (f32[160,1536]{1,0:T(8,128)S(1)}, f32[160,1536]{1,0:T(8,128)S(1)}, u32[]{:S(2)}, u32[]{:S(2)}) collective-permute-start(f32[160,1536]{1,0:T(8,128)S(1)} %convolution_multiply_fusion.2), channel_id=1, source_target_pairs={{0,24},{2,26},{4,28},{6,30},{8,0},{10,2},{12,4},{14,6},{16,8},{18,... | collective-permute-start | bytes 2949128 | tf_op jit(solution)/shard_map/ppermute | solution.py:15
  123.8 8.8 %convolution_multiply_fusion.4 = f32[16,1536]{1,0:T(8,128)S(1)} fusion(f32[16,3072]{1,0:T(8,128)S(1)} %collective-permute-done.4, f32[3072,1536]{1,0:T(8,128)} %param.4, f32[]{:T(128)} %bitcast), kind=kOutput, calls=%fused_computation.5 | convolution fusion | flops 453009408 | bytes 19169284 | tf_op jit(solution)/shard_map/dot_general | solution.py:23
  132.5 2.4 %collective-permute-done.5 = f32[176,1536]{1,0:T(8,128)S(1)} collective-permute-done((f32[176,1536]{1,0:T(8,128)S(1)}, f32[176,1536]{1,0:T(8,128)S(1)}, u32[]{:S(2)}, u32[]{:S(2)}) %collective-permute-start.5) | collective-permute-done | bytes 1081376 | tf_op jit(solution)/shard_map/ppermute | solution.py:15
  135.0 21.1 %collective-permute-done.6 = f32[160,1536]{1,0:T(8,128)S(1)} collective-permute-done((f32[160,1536]{1,0:T(8,128)S(1)}, f32[160,1536]{1,0:T(8,128)S(1)}, u32[]{:S(2)}, u32[]{:S(2)}) %collective-permute-start.6) | collective-permute-done | bytes 983072 | tf_op jit(solution)/shard_map/ppermute | solution.py:15
  156.0 1.7 %maximum_add_fusion = f32[384,1536]{1,0:T(8,128)} fusion(f32[384,1536]{1,0:T(8,128)S(1)} %convolution_multiply_fusion, f32[160,1536]{1,0:T(8,128)S(1)} %collective-permute-done.6, f32[176,1536]{1,0:T(8,128)S(1)} %collective-permute-done.5, f32[32,1536]{1,0:T(8,128)S(1)} %collective-permute-done.3, f32[384]{0:T(512)S(1)} %pad.3.clone), kind=kLoop, calls=%fused_computation.3 | loop fusion | flops 2359296 | bytes 6981120 | tf_op jit(solution)/shard_map/add | solution.py:55
  157.7 0.2 collective-permute-done.7
  158.0 0.7 fusion
  (7 shorter events, 0.1 us)
Async XLA Ops:
  0.0 5.9 %copy-start = (f32[384,3072]{1,0:T(8,128)S(1)}, f32[384,3072]{1,0:T(8,128)}, u32[]{:S(2)}) copy-start(f32[384,3072]{1,0:T(8,128)} %param.3) | copy-start | bytes 14155780
  1.2 23.4 %collective-permute-start = (f32[32,3072]{1,0:T(8,128)S(1)}, f32[32,3072]{1,0:T(8,128)S(1)}, u32[]{:S(2)}, u32[]{:S(2)}) collective-permute-start(f32[32,3072]{1,0:T(8,128)S(1)} %slice.15), channel_id=1, source_target_pairs={{0,14},{2,8},{4,10},{6,12},{8,22},{10,16},{12,18},{14,20},{16,30},... | collective-permute-start | bytes 1179656 | tf_op jit(solution)/shard_map/ppermute | solution.py:15
  4.9 56.9 %collective-permute-start.1 = (f32[176,3072]{1,0:T(8,128)S(1)}, f32[176,3072]{1,0:T(8,128)S(1)}, u32[]{:S(2)}, u32[]{:S(2)}) collective-permute-start(f32[176,3072]{1,0:T(8,128)S(1)} %slice.16), channel_id=1, source_target_pairs={{0,14},{2,8},{4,10},{6,12},{8,22},{10,16},{12,18},{14,20},{16,30},... | collective-permute-start | bytes 6488072 | tf_op jit(solution)/shard_map/ppermute | solution.py:15
  6.0 97.9 %collective-permute-start.2 = (f32[160,3072]{1,0:T(8,128)S(1)}, f32[160,3072]{1,0:T(8,128)S(1)}, u32[]{:S(2)}, u32[]{:S(2)}) collective-permute-start(f32[160,3072]{1,0:T(8,128)S(1)} %slice.17), channel_id=1, source_target_pairs={{0,14},{2,8},{4,10},{6,12},{8,22},{10,16},{12,18},{14,20},{16,30},... | collective-permute-start | bytes 5898248 | tf_op jit(solution)/shard_map/ppermute | solution.py:15
  8.0 98.8 %collective-permute-start.4 = (f32[16,3072]{1,0:T(8,128)S(1)}, f32[16,3072]{1,0:T(8,128)S(1)}, u32[]{:S(2)}, u32[]{:S(2)}) collective-permute-start(f32[16,3072]{1,0:T(8,128)S(1)} %slice.18), channel_id=1, source_target_pairs={{0,14},{2,8},{4,10},{6,12},{8,22},{10,16},{12,18},{14,20},{16,30},... | collective-permute-start | bytes 589832 | tf_op jit(solution)/shard_map/ppermute | solution.py:15
  103.9 7.9 %collective-permute-start.3 = (f32[32,1536]{1,0:T(8,128)S(1)}, f32[32,1536]{1,0:T(8,128)S(1)}, u32[]{:S(2)}, u32[]{:S(2)}) collective-permute-start(f32[32,1536]{1,0:T(8,128)S(1)} %convolution_multiply_fusion.3), channel_id=1, source_target_pairs={{0,24},{2,26},{4,28},{6,30},{8,0},{10,2},{12,4},{14,6},{16,8},{18,... | collective-permute-start | bytes 589832 | tf_op jit(solution)/shard_map/ppermute | solution.py:15
  106.8 28.2 %collective-permute-start.5 = (f32[176,1536]{1,0:T(8,128)S(1)}, f32[176,1536]{1,0:T(8,128)S(1)}, u32[]{:S(2)}, u32[]{:S(2)}) collective-permute-start(f32[176,1536]{1,0:T(8,128)S(1)} %convolution_multiply_fusion.1), channel_id=1, source_target_pairs={{0,24},{2,26},{4,28},{6,30},{8,0},{10,2},{12,4},{14,6},{16,8},{18,... | collective-permute-start | bytes 3244040 | tf_op jit(solution)/shard_map/ppermute | solution.py:15
  121.6 34.4 %collective-permute-start.6 = (f32[160,1536]{1,0:T(8,128)S(1)}, f32[160,1536]{1,0:T(8,128)S(1)}, u32[]{:S(2)}, u32[]{:S(2)}) collective-permute-start(f32[160,1536]{1,0:T(8,128)S(1)} %convolution_multiply_fusion.2), channel_id=1, source_target_pairs={{0,24},{2,26},{4,28},{6,30},{8,0},{10,2},{12,4},{14,6},{16,8},{18,... | collective-permute-start | bytes 2949128 | tf_op jit(solution)/shard_map/ppermute | solution.py:15
  132.5 25.5 %collective-permute-start.7 = (f32[16,1536]{1,0:T(8,128)S(1)}, f32[16,1536]{1,0:T(8,128)S(1)}, u32[]{:S(2)}, u32[]{:S(2)}) collective-permute-start(f32[16,1536]{1,0:T(8,128)S(1)} %convolution_multiply_fusion.4), channel_id=1, source_target_pairs={{0,24},{2,26},{4,28},{6,30},{8,0},{10,2},{12,4},{14,6},{16,8},{18,... | collective-permute-start | bytes 294920 | tf_op jit(solution)/shard_map/ppermute | solution.py:15

commit v3 on v2

--- a/solution.py
+++ b/solution.py
@@ -43,9 +43,9 @@
             total = shifted(total, -1, 0) + times_factor(visiting)
         return shifted(total, -1, 0)
 
-    own = times_factor(sigma_aa)
-    first_total = times_factor(after(first, own))
-    second_total = times_factor(after(second, first_total))
+    first_total = times_factor(first)
+    own = times_factor(after(sigma_aa, first_total))
+    second_total = times_factor(after(second, own))
     first_out = travel_back(after(first_total, second_total, third), 0)
     second_out = travel_back(after(second_total, last), 1)
     third_total = times_factor(after(third, last, first_out))

time: 159 us -> 159 us (level)
  waiting for transfers between devices: 87.9 us -> 79.6 us
  local copies, waits for them, and re-layouts: 3.15 us -> 8.93 us
  matrix products: 53.5 us -> 55.7 us
    ppermute x8, waiting for transfers between devices: 87.9 us -> 79.6 us  [shifted(): return lax.ppermute(block, ('row', 'col'), route)]
    slice x4, local copies, waits for them, and re-layouts: 3.07 us -> 8.83 us  [body(): piece, block = lax.optimization_barrier((block[start:end], block))]
    dot_general x5, matrix products: 53.5 us -> 55.7 us  [product(): jnp.dot(lhs_block, rhs_block, preferred_element_type=jnp.float32, precisi...]
  transfers between devices with their start and end apart: 8 -> 8, of which waited for: 7 -> 8; matrix products, arithmetic and copies ran while one was open for 36% -> 41% of each run, Pallas kernels for 0% -> 0%
where the time goes in v3:
time: 159 us; the launch traced here: 158 us
  waiting for transfers between devices  79.6 us (50%)
  matrix products  55.7 us (35%)
  starting transfers between devices  11.1 us (7%)
  local copies, waits for them, and re-layouts  8.93 us (6%)
  other arithmetic  2.45 us (2%)
    ppermute x8, waiting for transfers between devices, shifted(): return lax.ppermute(block, ('row', 'col'), route)  79.6 us
    dot_general x5, matrix products, product(): jnp.dot(lhs_block, rhs_block, preferred_element_type=jnp.float32, precisi...  55.7 us
    ppermute x8, starting transfers between devices, shifted(): return lax.ppermute(block, ('row', 'col'), route)  11.1 us
    slice x4, local copies, waits for them, and re-layouts, body(): piece, block = lax.optimization_barrier((block[start:end], block))  8.83 us
  transfers between devices with their start and end apart: 8, of which 8 were waited for; matrix products, arithmetic and copies ran while one was open for 41% of the time, Pallas kernels for 0%

profile of v3, /device:TPU:3, one launch (start us, length us, event | category | flops | bytes accessed | tf_op | source)
XLA Modules:
  0.0 158.5 jit_solution(7132720496609788584)
XLA Ops:
  0.0 1.0 slice.15
  1.0 1.9 %collective-permute-start = (f32[32,3072]{1,0:T(8,128)S(1)}, f32[32,3072]{1,0:T(8,128)S(1)}, u32[]{:S(2)}, u32[]{:S(2)}) collective-permute-start(f32[32,3072]{1,0:T(8,128)S(1)} %slice.15), channel_id=1, source_target_pairs={{0,14},{2,8},{4,10},{6,12},{8,22},{10,16},{12,18},{14,20},{16,30},... | collective-permute-start | bytes 1179656 | tf_op jit(solution)/shard_map/ppermute | solution.py:15
  2.9 3.2 %slice.16 = f32[176,3072]{1,0:T(8,128)} slice(f32[384,3072]{1,0:T(8,128)} %param.3), slice={[32:208], [0:3072]} | slice | bytes 4325376 | tf_op jit(solution)/shard_map/slice | solution.py:33
  6.1 1.0 collective-permute-start.1
  7.1 3.0 %slice.17 = f32[160,3072]{1,0:T(8,128)} slice(f32[384,3072]{1,0:T(8,128)} %param.3), slice={[208:368], [0:3072]} | slice | bytes 3932160 | tf_op jit(solution)/shard_map/slice | solution.py:33
  10.1 1.9 %collective-permute-start.2 = (f32[160,3072]{1,0:T(8,128)}, f32[160,3072]{1,0:T(8,128)}, u32[]{:S(2)}, u32[]{:S(2)}) collective-permute-start(f32[160,3072]{1,0:T(8,128)} %slice.17), channel_id=1, source_target_pairs={{0,14},{2,8},{4,10},{6,12},{8,22},{10,16},{12,18},{14,20},{16,30},... | collective-permute-start | bytes 5898248 | tf_op jit(solution)/shard_map/ppermute | solution.py:15
  12.0 1.6 %slice.18 = f32[16,3072]{1,0:T(8,128)} slice(f32[384,3072]{1,0:T(8,128)} %param.3), slice={[368:384], [0:3072]} | slice | bytes 393216 | tf_op jit(solution)/shard_map/slice | solution.py:33
  13.6 0.6 collective-permute-start.4
  15.3 10.2 %convolution_multiply_fusion.3 = f32[32,1536]{1,0:T(8,128)} fusion(f32[32,3072]{1,0:T(8,128)S(1)} %collective-permute-done, f32[3072,1536]{1,0:T(8,128)} %param.4, f32[]{:T(128)} %bitcast), kind=kOutput, calls=%fused_computation.4 | convolution fusion | flops 906018816 | bytes 19464196 | tf_op jit(solution)/shard_map/dot_general | solution.py:23
  25.5 17.0 %convolution_multiply_fusion = f32[384,1536]{1,0:T(8,128)S(1)} fusion(f32[384,3072]{1,0:T(8,128)} %param.3, f32[3072,1536]{1,0:T(8,128)} %param.4, f32[]{:T(128)} %bitcast), kind=kOutput, calls=%fused_computation | convolution fusion | flops 10872225792 | bytes 25952260 | tf_op jit(solution)/shard_map/dot_general | solution.py:23
  42.5 19.2 %collective-permute-done.1 = f32[176,3072]{1,0:T(8,128)} collective-permute-done((f32[176,3072]{1,0:T(8,128)}, f32[176,3072]{1,0:T(8,128)}, u32[]{:S(2)}, u32[]{:S(2)}) %collective-permute-start.1) | collective-permute-done | bytes 2162720 | tf_op jit(solution)/shard_map/ppermute | solution.py:15
  61.7 9.1 %convolution_multiply_fusion.1 = f32[176,1536]{1,0:T(8,128)S(1)} fusion(f32[176,3072]{1,0:T(8,128)} %collective-permute-done.1, f32[3072,1536]{1,0:T(8,128)S(1)} %bitcast.12, f32[]{:T(128)} %bitcast), kind=kOutput, calls=%fused_computation.1 | convolution fusion | flops 4983103488 | bytes 22118404 | tf_op jit(solution)/shard_map/dot_general | solution.py:23
  70.9 33.0 %collective-permute-done.2 = f32[160,3072]{1,0:T(8,128)} collective-permute-done((f32[160,3072]{1,0:T(8,128)}, f32[160,3072]{1,0:T(8,128)}, u32[]{:S(2)}, u32[]{:S(2)}) %collective-permute-start.2) | collective-permute-done | bytes 1966112 | tf_op jit(solution)/shard_map/ppermute | solution.py:15
  103.8 1.4 collective-permute-start.3
  105.3 1.3 collective-permute-done.4
  106.6 1.9 %collective-permute-start.5 = (f32[176,1536]{1,0:T(8,128)S(1)}, f32[176,1536]{1,0:T(8,128)S(1)}, u32[]{:S(2)}, u32[]{:S(2)}) collective-permute-start(f32[176,1536]{1,0:T(8,128)S(1)} %convolution_multiply_fusion.1), channel_id=1, source_target_pairs={{0,24},{2,26},{4,28},{6,30},{8,0},{10,2},{12,4},{14,6},{16,8},{18,... | collective-permute-start | bytes 3244040 | tf_op jit(solution)/shard_map/ppermute | solution.py:15
  108.5 3.2 %collective-permute-done.3 = f32[32,1536]{1,0:T(8,128)S(1)} collective-permute-done((f32[32,1536]{1,0:T(8,128)}, f32[32,1536]{1,0:T(8,128)S(1)}, u32[]{:S(2)}, u32[]{:S(2)}) %collective-permute-start.3) | collective-permute-done | bytes 196640 | tf_op jit(solution)/shard_map/ppermute | solution.py:15
  111.6 10.4 %convolution_multiply_fusion.2 = f32[160,1536]{1,0:T(8,128)S(1)} fusion(f32[160,3072]{1,0:T(8,128)} %collective-permute-done.2, f32[3072,1536]{1,0:T(8,128)} %param.4, f32[]{:T(128)} %bitcast), kind=kOutput, calls=%fused_computation.2 | convolution fusion | flops 4530094080 | bytes 21823492 | tf_op jit(solution)/shard_map/dot_general | solution.py:23
  122.1 2.4 %collective-permute-start.6 = (f32[160,1536]{1,0:T(8,128)S(1)}, f32[160,1536]{1,0:T(8,128)S(1)}, u32[]{:S(2)}, u32[]{:S(2)}) collective-permute-start(f32[160,1536]{1,0:T(8,128)S(1)} %convolution_multiply_fusion.2), channel_id=1, source_target_pairs={{0,24},{2,26},{4,28},{6,30},{8,0},{10,2},{12,4},{14,6},{16,8},{18,... | collective-permute-start | bytes 2949128 | tf_op jit(solution)/shard_map/ppermute | solution.py:15
  124.5 8.9 %convolution_multiply_fusion.4 = f32[16,1536]{1,0:T(8,128)S(1)} fusion(f32[16,3072]{1,0:T(8,128)S(1)} %collective-permute-done.4, f32[3072,1536]{1,0:T(8,128)} %param.4, f32[]{:T(128)} %bitcast), kind=kOutput, calls=%fused_computation.5 | convolution fusion | flops 453009408 | bytes 19169284 | tf_op jit(solution)/shard_map/dot_general | solution.py:23
  133.5 1.3 collective-permute-done.5
  134.8 21.1 %collective-permute-done.6 = f32[160,1536]{1,0:T(8,128)S(1)} collective-permute-done((f32[160,1536]{1,0:T(8,128)S(1)}, f32[160,1536]{1,0:T(8,128)S(1)}, u32[]{:S(2)}, u32[]{:S(2)}) %collective-permute-start.6) | collective-permute-done | bytes 983072 | tf_op jit(solution)/shard_map/ppermute | solution.py:15
  155.9 1.8 %maximum_add_fusion = f32[384,1536]{1,0:T(8,128)} fusion(f32[384,1536]{1,0:T(8,128)S(1)} %convolution_multiply_fusion, f32[160,1536]{1,0:T(8,128)S(1)} %collective-permute-done.6, f32[176,1536]{1,0:T(8,128)S(1)} %collective-permute-done.5, f32[32,1536]{1,0:T(8,128)S(1)} %collective-permute-done.3, f32[384]{0:T(512)S(1)} %pad.3.clone), kind=kLoop, calls=%fused_computation.3 | loop fusion | flops 2359296 | bytes 6981120 | tf_op jit(solution)/shard_map/add | solution.py:55
  157.8 0.7 fusion
  (16 shorter events, 0.7 us)
Async XLA Ops:
  1.0 14.2 %collective-permute-start = (f32[32,3072]{1,0:T(8,128)S(1)}, f32[32,3072]{1,0:T(8,128)S(1)}, u32[]{:S(2)}, u32[]{:S(2)}) collective-permute-start(f32[32,3072]{1,0:T(8,128)S(1)} %slice.15), channel_id=1, source_target_pairs={{0,14},{2,8},{4,10},{6,12},{8,22},{10,16},{12,18},{14,20},{16,30},... | collective-permute-start | bytes 1179656 | tf_op jit(solution)/shard_map/ppermute | solution.py:15
  6.1 55.6 %collective-permute-start.1 = (f32[176,3072]{1,0:T(8,128)}, f32[176,3072]{1,0:T(8,128)}, u32[]{:S(2)}, u32[]{:S(2)}) collective-permute-start(f32[176,3072]{1,0:T(8,128)} %slice.16), channel_id=1, source_target_pairs={{0,14},{2,8},{4,10},{6,12},{8,22},{10,16},{12,18},{14,20},{16,30},... | collective-permute-start | bytes 6488072 | tf_op jit(solution)/shard_map/ppermute | solution.py:15
  10.1 93.7 %collective-permute-start.2 = (f32[160,3072]{1,0:T(8,128)}, f32[160,3072]{1,0:T(8,128)}, u32[]{:S(2)}, u32[]{:S(2)}) collective-permute-start(f32[160,3072]{1,0:T(8,128)} %slice.17), channel_id=1, source_target_pairs={{0,14},{2,8},{4,10},{6,12},{8,22},{10,16},{12,18},{14,20},{16,30},... | collective-permute-start | bytes 5898248 | tf_op jit(solution)/shard_map/ppermute | solution.py:15
  13.6 93.0 %collective-permute-start.4 = (f32[16,3072]{1,0:T(8,128)}, f32[16,3072]{1,0:T(8,128)S(1)}, u32[]{:S(2)}, u32[]{:S(2)}) collective-permute-start(f32[16,3072]{1,0:T(8,128)} %slice.18), channel_id=1, source_target_pairs={{0,14},{2,8},{4,10},{6,12},{8,22},{10,16},{12,18},{14,20},{16,30},... | collective-permute-start | bytes 589832 | tf_op jit(solution)/shard_map/ppermute | solution.py:15
  15.2 46.5 %slice-start = ((s8[18874368]{0:T(1024)(128)(4,1)}), s8[4194304]{0:T(1024)(128)(4,1)S(1)}, s32[]{:S(2)}) async-start(s8[18874368]{0:T(1024)(128)(4,1)} %bitcast.11), calls=%async_computation | async-start | bytes 8388608
  15.3 46.5 %slice-start.1 = ((s8[18874368]{0:T(1024)(128)(4,1)}), s8[4194304]{0:T(1024)(128)(4,1)S(1)}, s32[]{:S(2)}) async-start(s8[18874368]{0:T(1024)(128)(4,1)} %bitcast.11), calls=%async_computation.1 | async-start | bytes 8388608
  15.3 46.5 %slice-start.2 = ((s8[18874368]{0:T(1024)(128)(4,1)}), s8[2097152]{0:T(1024)(128)(4,1)S(1)}, s32[]{:S(2)}) async-start(s8[18874368]{0:T(1024)(128)(4,1)} %bitcast.11), calls=%async_computation.2 | async-start | bytes 4194304
  25.5 36.2 %slice-start.3 = ((s8[18874368]{0:T(1024)(128)(4,1)}), s8[4194304]{0:T(1024)(128)(4,1)S(1)}, s32[]{:S(2)}) async-start(s8[18874368]{0:T(1024)(128)(4,1)} %bitcast.11), calls=%async_computation.3 | async-start | bytes 8388608
  25.5 36.2 %slice-start.4 = ((s8[18874368]{0:T(1024)(128)(4,1)}), s8[4194304]{0:T(1024)(128)(4,1)S(1)}, s32[]{:S(2)}) async-start(s8[18874368]{0:T(1024)(128)(4,1)} %bitcast.11), calls=%async_computation.4 | async-start | bytes 8388608
  103.8 7.8 %collective-permute-start.3 = (f32[32,1536]{1,0:T(8,128)}, f32[32,1536]{1,0:T(8,128)S(1)}, u32[]{:S(2)}, u32[]{:S(2)}) collective-permute-start(f32[32,1536]{1,0:T(8,128)} %convolution_multiply_fusion.3), channel_id=1, source_target_pairs={{0,24},{2,26},{4,28},{6,30},{8,0},{10,2},{12,4},{14,6},{16,8},{18,... | collective-permute-start | bytes 589832 | tf_op jit(solution)/shard_map/ppermute | solution.py:15
  106.6 28.2 %collective-permute-start.5 = (f32[176,1536]{1,0:T(8,128)S(1)}, f32[176,1536]{1,0:T(8,128)S(1)}, u32[]{:S(2)}, u32[]{:S(2)}) collective-permute-start(f32[176,1536]{1,0:T(8,128)S(1)} %convolution_multiply_fusion.1), channel_id=1, source_target_pairs={{0,24},{2,26},{4,28},{6,30},{8,0},{10,2},{12,4},{14,6},{16,8},{18,... | collective-permute-start | bytes 3244040 | tf_op jit(solution)/shard_map/ppermute | solution.py:15
  122.1 33.8 %collective-permute-start.6 = (f32[160,1536]{1,0:T(8,128)S(1)}, f32[160,1536]{1,0:T(8,128)S(1)}, u32[]{:S(2)}, u32[]{:S(2)}) collective-permute-start(f32[160,1536]{1,0:T(8,128)S(1)} %convolution_multiply_fusion.2), channel_id=1, source_target_pairs={{0,24},{2,26},{4,28},{6,30},{8,0},{10,2},{12,4},{14,6},{16,8},{18,... | collective-permute-start | bytes 2949128 | tf_op jit(solution)/shard_map/ppermute | solution.py:15
  133.5 24.4 %collective-permute-start.7 = (f32[16,1536]{1,0:T(8,128)S(1)}, f32[16,1536]{1,0:T(8,128)S(1)}, u32[]{:S(2)}, u32[]{:S(2)}) collective-permute-start(f32[16,1536]{1,0:T(8,128)S(1)} %convolution_multiply_fusion.4), channel_id=1, source_target_pairs={{0,24},{2,26},{4,28},{6,30},{8,0},{10,2},{12,4},{14,6},{16,8},{18,... | collective-permute-start | bytes 294920 | tf_op jit(solution)/shard_map/ppermute | solution.py:15

commit v4 on v3

--- a/solution.py
+++ b/solution.py
@@ -4,7 +4,7 @@
 from jax.sharding import PartitionSpec as P
 
 
-CUTS = (0, 4, 26, 46, 48)
+CUTS = (0, 4, 27, 46, 48)
 
 
 def shifted(block, rows_by, cols_by):
@@ -47,7 +47,7 @@
     own = times_factor(after(sigma_aa, first_total))
     second_total = times_factor(after(second, own))
     first_out = travel_back(after(first_total, second_total, third), 0)
-    second_out = travel_back(after(second_total, last), 1)
+    second_out = travel_back(after(second_total, third), 1)
     third_total = times_factor(after(third, last, first_out))
     third_out = travel_back(third_total, 2)
     last_out = travel_back(times_factor(after(last, third_total)), 3)

time: 159 us -> 159 us (level)
  waiting for transfers between devices: 79.6 us -> 81.3 us
  starting transfers between devices: 11.1 us -> 9.4 us
    ppermute x8, starting transfers between devices: 11.1 us -> 9.4 us  [shifted(): return lax.ppermute(block, ('row', 'col'), route)]
    ppermute x8, waiting for transfers between devices: 79.6 us -> 81.3 us  [shifted(): return lax.ppermute(block, ('row', 'col'), route)]
  transfers between devices with their start and end apart: 8 -> 8, of which waited for: 8 -> 7; matrix products, arithmetic and copies ran while one was open for 41% -> 41% of each run, Pallas kernels for 0% -> 0%
where the time goes in v4:
time: 159 us; the launch traced here: 158 us
  waiting for transfers between devices  81.3 us (51%)
  matrix products  55.7 us (35%)
  starting transfers between devices  9.4 us (6%)
  local copies, waits for them, and re-layouts  8.91 us (6%)
  other arithmetic  2.45 us (2%)
    ppermute x8, waiting for transfers between devices, shifted(): return lax.ppermute(block, ('row', 'col'), route)  81.3 us
    dot_general x5, matrix products, product(): jnp.dot(lhs_block, rhs_block, preferred_element_type=jnp.float32, precisi...  55.7 us
    ppermute x8, starting transfers between devices, shifted(): return lax.ppermute(block, ('row', 'col'), route)  9.4 us
    slice x4, local copies, waits for them, and re-layouts, body(): piece, block = lax.optimization_barrier((block[start:end], block))  8.82 us
  transfers between devices with their start and end apart: 8, of which 7 were waited for; matrix products, arithmetic and copies ran while one was open for 41% of the time, Pallas kernels for 0%

profile of v4, /device:TPU:3, one launch (start us, length us, event | category | flops | bytes accessed | tf_op | source)
XLA Modules:
  0.0 158.5 jit_solution(13984916702390953432)
XLA Ops:
  0.0 1.0 slice.15
  1.0 1.9 %collective-permute-start = (f32[32,3072]{1,0:T(8,128)S(1)}, f32[32,3072]{1,0:T(8,128)S(1)}, u32[]{:S(2)}, u32[]{:S(2)}) collective-permute-start(f32[32,3072]{1,0:T(8,128)S(1)} %slice.15), channel_id=1, source_target_pairs={{0,14},{2,8},{4,10},{6,12},{8,22},{10,16},{12,18},{14,20},{16,30},... | collective-permute-start | bytes 1179656 | tf_op jit(solution)/shard_map/ppermute | solution.py:15
  2.9 3.2 %slice.16 = f32[184,3072]{1,0:T(8,128)} slice(f32[384,3072]{1,0:T(8,128)} %param.3), slice={[32:216], [0:3072]} | slice | bytes 4521984 | tf_op jit(solution)/shard_map/slice | solution.py:33
  6.2 1.0 collective-permute-start.1
  7.2 2.9 %slice.17 = f32[152,3072]{1,0:T(8,128)} slice(f32[384,3072]{1,0:T(8,128)} %param.3), slice={[216:368], [0:3072]} | slice | bytes 3735552 | tf_op jit(solution)/shard_map/slice | solution.py:33
  10.1 1.9 %collective-permute-start.2 = (f32[152,3072]{1,0:T(8,128)}, f32[152,3072]{1,0:T(8,128)}, u32[]{:S(2)}, u32[]{:S(2)}) collective-permute-start(f32[152,3072]{1,0:T(8,128)} %slice.17), channel_id=1, source_target_pairs={{0,14},{2,8},{4,10},{6,12},{8,22},{10,16},{12,18},{14,20},{16,30},... | collective-permute-start | bytes 5603336 | tf_op jit(solution)/shard_map/ppermute | solution.py:15
  12.0 1.6 %slice.18 = f32[16,3072]{1,0:T(8,128)} slice(f32[384,3072]{1,0:T(8,128)} %param.3), slice={[368:384], [0:3072]} | slice | bytes 393216 | tf_op jit(solution)/shard_map/slice | solution.py:33
  13.6 0.6 collective-permute-start.5
  14.8 0.4 collective-permute-done
  15.3 10.2 %convolution_multiply_fusion.3 = f32[32,1536]{1,0:T(8,128)} fusion(f32[32,3072]{1,0:T(8,128)S(1)} %collective-permute-done, f32[3072,1536]{1,0:T(8,128)} %param.4, f32[]{:T(128)} %bitcast), kind=kOutput, calls=%fused_computation.4 | convolution fusion | flops 906018816 | bytes 19464196 | tf_op jit(solution)/shard_map/dot_general | solution.py:23
  25.5 17.0 %convolution_multiply_fusion = f32[384,1536]{1,0:T(8,128)S(1)} fusion(f32[384,3072]{1,0:T(8,128)} %param.3, f32[3072,1536]{1,0:T(8,128)} %param.4, f32[]{:T(128)} %bitcast), kind=kOutput, calls=%fused_computation | convolution fusion | flops 10872225792 | bytes 25952260 | tf_op jit(solution)/shard_map/dot_general | solution.py:23
  42.4 21.4 %collective-permute-done.1 = f32[184,3072]{1,0:T(8,128)} collective-permute-done((f32[184,3072]{1,0:T(8,128)}, f32[184,3072]{1,0:T(8,128)}, u32[]{:S(2)}, u32[]{:S(2)}) %collective-permute-start.1) | collective-permute-done | bytes 2261024 | tf_op jit(solution)/shard_map/ppermute | solution.py:15
  63.8 9.5 %convolution_multiply_fusion.1 = f32[184,1536]{1,0:T(8,128)S(1)} fusion(f32[184,3072]{1,0:T(8,128)} %collective-permute-done.1, f32[3072,1536]{1,0:T(8,128)S(1)} %bitcast.12, f32[]{:T(128)} %bitcast), kind=kOutput, calls=%fused_computation.1 | convolution fusion | flops 5209608192 | bytes 22265860 | tf_op jit(solution)/shard_map/dot_general | solution.py:23
  73.3 30.5 %collective-permute-done.2 = f32[152,3072]{1,0:T(8,128)} collective-permute-done((f32[152,3072]{1,0:T(8,128)}, f32[152,3072]{1,0:T(8,128)}, u32[]{:S(2)}, u32[]{:S(2)}) %collective-permute-start.2) | collective-permute-done | bytes 1867808 | tf_op jit(solution)/shard_map/ppermute | solution.py:15
  103.8 1.4 collective-permute-start.3
  105.3 0.2 collective-permute-start.4
  105.5 1.1 collective-permute-done.5
  106.6 5.0 %collective-permute-done.3 = f32[32,1536]{1,0:T(8,128)S(1)} collective-permute-done((f32[32,1536]{1,0:T(8,128)}, f32[32,1536]{1,0:T(8,128)S(1)}, u32[]{:S(2)}, u32[]{:S(2)}) %collective-permute-start.3) | collective-permute-done | bytes 196640 | tf_op jit(solution)/shard_map/ppermute | solution.py:15
  111.6 10.2 %convolution_multiply_fusion.2 = f32[152,1536]{1,0:T(8,128)S(1)} fusion(f32[152,3072]{1,0:T(8,128)} %collective-permute-done.2, f32[3072,1536]{1,0:T(8,128)} %param.4, f32[]{:T(128)} %bitcast), kind=kOutput, calls=%fused_computation.2 | convolution fusion | flops 4303589376 | bytes 21676036 | tf_op jit(solution)/shard_map/dot_general | solution.py:23
  121.8 2.4 %collective-permute-start.6 = (f32[152,1536]{1,0:T(8,128)S(1)}, f32[152,1536]{1,0:T(8,128)S(1)}, u32[]{:S(2)}, u32[]{:S(2)}) collective-permute-start(f32[152,1536]{1,0:T(8,128)S(1)} %convolution_multiply_fusion.2), channel_id=1, source_target_pairs={{0,24},{2,26},{4,28},{6,30},{8,0},{10,2},{12,4},{14,6},{16,8},{18,... | collective-permute-start | bytes 2801672 | tf_op jit(solution)/shard_map/ppermute | solution.py:15
  124.3 8.9 %convolution_multiply_fusion.4 = f32[16,1536]{1,0:T(8,128)S(1)} fusion(f32[16,3072]{1,0:T(8,128)S(1)} %collective-permute-done.5, f32[3072,1536]{1,0:T(8,128)} %param.4, f32[]{:T(128)} %bitcast), kind=kOutput, calls=%fused_computation.5 | convolution fusion | flops 453009408 | bytes 19169284 | tf_op jit(solution)/shard_map/dot_general | solution.py:23
  133.2 22.6 %collective-permute-done.6 = f32[152,1536]{1,0:T(8,128)S(1)} collective-permute-done((f32[152,1536]{1,0:T(8,128)S(1)}, f32[152,1536]{1,0:T(8,128)S(1)}, u32[]{:S(2)}, u32[]{:S(2)}) %collective-permute-start.6) | collective-permute-done | bytes 933920 | tf_op jit(solution)/shard_map/ppermute | solution.py:15
  155.9 1.8 %maximum_add_fusion = f32[384,1536]{1,0:T(8,128)} fusion(f32[384,1536]{1,0:T(8,128)S(1)} %convolution_multiply_fusion, f32[152,1536]{1,0:T(8,128)S(1)} %collective-permute-done.6, f32[184,1536]{1,0:T(8,128)S(1)} %collective-permute-done.4, f32[32,1536]{1,0:T(8,128)S(1)} %collective-permute-done.3, f32[384]{0:T(512)S(1)} %pad.3.clone), kind=kLoop, calls=%fused_computation.3 | loop fusion | flops 2359296 | bytes 6981120 | tf_op jit(solution)/shard_map/add | solution.py:55
  157.8 0.7 fusion
  (16 shorter events, 0.3 us)
Async XLA Ops:
  1.0 14.2 %collective-permute-start = (f32[32,3072]{1,0:T(8,128)S(1)}, f32[32,3072]{1,0:T(8,128)S(1)}, u32[]{:S(2)}, u32[]{:S(2)}) collective-permute-start(f32[32,3072]{1,0:T(8,128)S(1)} %slice.15), channel_id=1, source_target_pairs={{0,14},{2,8},{4,10},{6,12},{8,22},{10,16},{12,18},{14,20},{16,30},... | collective-permute-start | bytes 1179656 | tf_op jit(solution)/shard_map/ppermute | solution.py:15
  6.2 57.6 %collective-permute-start.1 = (f32[184,3072]{1,0:T(8,128)}, f32[184,3072]{1,0:T(8,128)}, u32[]{:S(2)}, u32[]{:S(2)}) collective-permute-start(f32[184,3072]{1,0:T(8,128)} %slice.16), channel_id=1, source_target_pairs={{0,14},{2,8},{4,10},{6,12},{8,22},{10,16},{12,18},{14,20},{16,30},... | collective-permute-start | bytes 6782984 | tf_op jit(solution)/shard_map/ppermute | solution.py:15
  10.1 93.7 %collective-permute-start.2 = (f32[152,3072]{1,0:T(8,128)}, f32[152,3072]{1,0:T(8,128)}, u32[]{:S(2)}, u32[]{:S(2)}) collective-permute-start(f32[152,3072]{1,0:T(8,128)} %slice.17), channel_id=1, source_target_pairs={{0,14},{2,8},{4,10},{6,12},{8,22},{10,16},{12,18},{14,20},{16,30},... | collective-permute-start | bytes 5603336 | tf_op jit(solution)/shard_map/ppermute | solution.py:15
  13.6 93.0 %collective-permute-start.5 = (f32[16,3072]{1,0:T(8,128)}, f32[16,3072]{1,0:T(8,128)S(1)}, u32[]{:S(2)}, u32[]{:S(2)}) collective-permute-start(f32[16,3072]{1,0:T(8,128)} %slice.18), channel_id=1, source_target_pairs={{0,14},{2,8},{4,10},{6,12},{8,22},{10,16},{12,18},{14,20},{16,30},... | collective-permute-start | bytes 589832 | tf_op jit(solution)/shard_map/ppermute | solution.py:15
  15.2 48.6 %slice-start = ((s8[18874368]{0:T(1024)(128)(4,1)}), s8[4194304]{0:T(1024)(128)(4,1)S(1)}, s32[]{:S(2)}) async-start(s8[18874368]{0:T(1024)(128)(4,1)} %bitcast.11), calls=%async_computation | async-start | bytes 8388608
  15.3 48.6 %slice-start.1 = ((s8[18874368]{0:T(1024)(128)(4,1)}), s8[4194304]{0:T(1024)(128)(4,1)S(1)}, s32[]{:S(2)}) async-start(s8[18874368]{0:T(1024)(128)(4,1)} %bitcast.11), calls=%async_computation.1 | async-start | bytes 8388608
  15.3 48.6 %slice-start.2 = ((s8[18874368]{0:T(1024)(128)(4,1)}), s8[2097152]{0:T(1024)(128)(4,1)S(1)}, s32[]{:S(2)}) async-start(s8[18874368]{0:T(1024)(128)(4,1)} %bitcast.11), calls=%async_computation.2 | async-start | bytes 4194304
  25.5 38.3 %slice-start.3 = ((s8[18874368]{0:T(1024)(128)(4,1)}), s8[4194304]{0:T(1024)(128)(4,1)S(1)}, s32[]{:S(2)}) async-start(s8[18874368]{0:T(1024)(128)(4,1)} %bitcast.11), calls=%async_computation.3 | async-start | bytes 8388608
  25.5 38.4 %slice-start.4 = ((s8[18874368]{0:T(1024)(128)(4,1)}), s8[4194304]{0:T(1024)(128)(4,1)S(1)}, s32[]{:S(2)}) async-start(s8[18874368]{0:T(1024)(128)(4,1)} %bitcast.11), calls=%async_computation.4 | async-start | bytes 8388608
  103.8 7.8 %collective-permute-start.3 = (f32[32,1536]{1,0:T(8,128)}, f32[32,1536]{1,0:T(8,128)S(1)}, u32[]{:S(2)}, u32[]{:S(2)}) collective-permute-start(f32[32,1536]{1,0:T(8,128)} %convolution_multiply_fusion.3), channel_id=1, source_target_pairs={{0,24},{2,26},{4,28},{6,30},{8,0},{10,2},{12,4},{14,6},{16,8},{18,... | collective-permute-start | bytes 589832 | tf_op jit(solution)/shard_map/ppermute | solution.py:15
  105.3 50.6 %collective-permute-start.4 = (f32[184,1536]{1,0:T(8,128)S(1)}, f32[184,1536]{1,0:T(8,128)S(1)}, u32[]{:S(2)}, u32[]{:S(2)}) collective-permute-start(f32[184,1536]{1,0:T(8,128)S(1)} %convolution_multiply_fusion.1), channel_id=1, source_target_pairs={{0,24},{2,26},{4,28},{6,30},{8,0},{10,2},{12,4},{14,6},{16,8},{18,... | collective-permute-start | bytes 3391496 | tf_op jit(solution)/shard_map/ppermute | solution.py:15
  121.8 34.1 %collective-permute-start.6 = (f32[152,1536]{1,0:T(8,128)S(1)}, f32[152,1536]{1,0:T(8,128)S(1)}, u32[]{:S(2)}, u32[]{:S(2)}) collective-permute-start(f32[152,1536]{1,0:T(8,128)S(1)} %convolution_multiply_fusion.2), channel_id=1, source_target_pairs={{0,24},{2,26},{4,28},{6,30},{8,0},{10,2},{12,4},{14,6},{16,8},{18,... | collective-permute-start | bytes 2801672 | tf_op jit(solution)/shard_map/ppermute | solution.py:15
  133.2 24.6 %collective-permute-start.7 = (f32[16,1536]{1,0:T(8,128)S(1)}, f32[16,1536]{1,0:T(8,128)S(1)}, u32[]{:S(2)}, u32[]{:S(2)}) collective-permute-start(f32[16,1536]{1,0:T(8,128)S(1)} %convolution_multiply_fusion.4), channel_id=1, source_target_pairs={{0,24},{2,26},{4,28},{6,30},{8,0},{10,2},{12,4},{14,6},{16,8},{18,... | collective-permute-start | bytes 294920 | tf_op jit(solution)/shard_map/ppermute | solution.py:15

commit v5 on v4

--- a/solution.py
+++ b/solution.py
@@ -4,7 +4,7 @@
 from jax.sharding import PartitionSpec as P
 
 
-CUTS = (0, 4, 27, 46, 48)
+CUTS = (0, 4, 28, 46, 48)
 
 
 def shifted(block, rows_by, cols_by):

time: 159 us -> 159 us (level)
  no operation moved by 1% of the time
where the time goes in v5:
time: 159 us; the launch traced here: 158 us
  waiting for transfers between devices  81.2 us (51%)
  matrix products  55.8 us (35%)
  starting transfers between devices  9.39 us (6%)
  local copies, waits for them, and re-layouts  8.9 us (6%)
  other arithmetic  2.45 us (2%)
    ppermute x8, waiting for transfers between devices, shifted(): return lax.ppermute(block, ('row', 'col'), route)  81.2 us
    dot_general x5, matrix products, product(): jnp.dot(lhs_block, rhs_block, preferred_element_type=jnp.float32, precisi...  55.8 us
    ppermute x8, starting transfers between devices, shifted(): return lax.ppermute(block, ('row', 'col'), route)  9.39 us
    slice x4, local copies, waits for them, and re-layouts, body(): piece, block = lax.optimization_barrier((block[start:end], block))  8.8 us
  transfers between devices with their start and end apart: 8, of which 7 were waited for; matrix products, arithmetic and copies ran while one was open for 41% of the time, Pallas kernels for 0%

profile of v5, /device:TPU:3, one launch (start us, length us, event | category | flops | bytes accessed | tf_op | source)
XLA Modules:
  0.0 158.5 jit_solution(6928903703526630420)
XLA Ops:
  0.0 1.0 slice.15
  1.0 1.9 %collective-permute-start = (f32[32,3072]{1,0:T(8,128)S(1)}, f32[32,3072]{1,0:T(8,128)S(1)}, u32[]{:S(2)}, u32[]{:S(2)}) collective-permute-start(f32[32,3072]{1,0:T(8,128)S(1)} %slice.15), channel_id=1, source_target_pairs={{0,14},{2,8},{4,10},{6,12},{8,22},{10,16},{12,18},{14,20},{16,30},... | collective-permute-start | bytes 1179656 | tf_op jit(solution)/shard_map/ppermute | solution.py:15
  2.9 3.3 %slice.16 = f32[192,3072]{1,0:T(8,128)} slice(f32[384,3072]{1,0:T(8,128)} %param.3), slice={[32:224], [0:3072]} | slice | bytes 4718592 | tf_op jit(solution)/shard_map/slice | solution.py:33
  6.2 1.0 collective-permute-start.1
  7.2 2.9 %slice.17 = f32[144,3072]{1,0:T(8,128)} slice(f32[384,3072]{1,0:T(8,128)} %param.3), slice={[224:368], [0:3072]} | slice | bytes 3538944 | tf_op jit(solution)/shard_map/slice | solution.py:33
  10.1 1.9 %collective-permute-start.2 = (f32[144,3072]{1,0:T(8,128)}, f32[144,3072]{1,0:T(8,128)}, u32[]{:S(2)}, u32[]{:S(2)}) collective-permute-start(f32[144,3072]{1,0:T(8,128)} %slice.17), channel_id=1, source_target_pairs={{0,14},{2,8},{4,10},{6,12},{8,22},{10,16},{12,18},{14,20},{16,30},... | collective-permute-start | bytes 5308424 | tf_op jit(solution)/shard_map/ppermute | solution.py:15
  11.9 1.6 %slice.18 = f32[16,3072]{1,0:T(8,128)} slice(f32[384,3072]{1,0:T(8,128)} %param.3), slice={[368:384], [0:3072]} | slice | bytes 393216 | tf_op jit(solution)/shard_map/slice | solution.py:33
  13.6 0.6 collective-permute-start.5
  14.8 0.4 collective-permute-done
  15.3 10.2 %convolution_multiply_fusion.3 = f32[32,1536]{1,0:T(8,128)} fusion(f32[32,3072]{1,0:T(8,128)S(1)} %collective-permute-done, f32[3072,1536]{1,0:T(8,128)} %param.4, f32[]{:T(128)} %bitcast), kind=kOutput, calls=%fused_computation.4 | convolution fusion | flops 906018816 | bytes 19464196 | tf_op jit(solution)/shard_map/dot_general | solution.py:23
  25.5 17.0 %convolution_multiply_fusion = f32[384,1536]{1,0:T(8,128)S(1)} fusion(f32[384,3072]{1,0:T(8,128)} %param.3, f32[3072,1536]{1,0:T(8,128)} %param.4, f32[]{:T(128)} %bitcast), kind=kOutput, calls=%fused_computation | convolution fusion | flops 10872225792 | bytes 25952260 | tf_op jit(solution)/shard_map/dot_general | solution.py:23
  42.5 23.5 %collective-permute-done.1 = f32[192,3072]{1,0:T(8,128)} collective-permute-done((f32[192,3072]{1,0:T(8,128)}, f32[192,3072]{1,0:T(8,128)}, u32[]{:S(2)}, u32[]{:S(2)}) %collective-permute-start.1) | collective-permute-done | bytes 2359328 | tf_op jit(solution)/shard_map/ppermute | solution.py:15
  66.0 9.7 %convolution_multiply_fusion.1 = f32[192,1536]{1,0:T(8,128)S(1)} fusion(f32[192,3072]{1,0:T(8,128)} %collective-permute-done.1, f32[3072,1536]{1,0:T(8,128)S(1)} %bitcast.12, f32[]{:T(128)} %bitcast), kind=kOutput, calls=%fused_computation.1 | convolution fusion | flops 5436112896 | bytes 22413316 | tf_op jit(solution)/shard_map/dot_general | solution.py:23
  75.6 28.2 %collective-permute-done.2 = f32[144,3072]{1,0:T(8,128)} collective-permute-done((f32[144,3072]{1,0:T(8,128)}, f32[144,3072]{1,0:T(8,128)}, u32[]{:S(2)}, u32[]{:S(2)}) %collective-permute-start.2) | collective-permute-done | bytes 1769504 | tf_op jit(solution)/shard_map/ppermute | solution.py:15
  103.8 1.4 collective-permute-start.3
  105.3 0.2 collective-permute-start.4
  105.5 1.2 collective-permute-done.5
  106.7 4.9 %collective-permute-done.3 = f32[32,1536]{1,0:T(8,128)S(1)} collective-permute-done((f32[32,1536]{1,0:T(8,128)}, f32[32,1536]{1,0:T(8,128)S(1)}, u32[]{:S(2)}, u32[]{:S(2)}) %collective-permute-start.3) | collective-permute-done | bytes 196640 | tf_op jit(solution)/shard_map/ppermute | solution.py:15
  111.6 10.0 %convolution_multiply_fusion.2 = f32[144,1536]{1,0:T(8,128)S(1)} fusion(f32[144,3072]{1,0:T(8,128)} %collective-permute-done.2, f32[3072,1536]{1,0:T(8,128)} %param.4, f32[]{:T(128)} %bitcast), kind=kOutput, calls=%fused_computation.2 | convolution fusion | flops 4077084672 | bytes 21528580 | tf_op jit(solution)/shard_map/dot_general | solution.py:23
  121.6 2.4 %collective-permute-start.6 = (f32[144,1536]{1,0:T(8,128)S(1)}, f32[144,1536]{1,0:T(8,128)S(1)}, u32[]{:S(2)}, u32[]{:S(2)}) collective-permute-start(f32[144,1536]{1,0:T(8,128)S(1)} %convolution_multiply_fusion.2), channel_id=1, source_target_pairs={{0,24},{2,26},{4,28},{6,30},{8,0},{10,2},{12,4},{14,6},{16,8},{18,... | collective-permute-start | bytes 2654216 | tf_op jit(solution)/shard_map/ppermute | solution.py:15
  124.1 9.0 %convolution_multiply_fusion.4 = f32[16,1536]{1,0:T(8,128)S(1)} fusion(f32[16,3072]{1,0:T(8,128)} %collective-permute-done.5, f32[3072,1536]{1,0:T(8,128)} %param.4, f32[]{:T(128)} %bitcast), kind=kOutput, calls=%fused_computation.5 | convolution fusion | flops 453009408 | bytes 19169284 | tf_op jit(solution)/shard_map/dot_general | solution.py:23
  133.1 22.7 %collective-permute-done.6 = f32[144,1536]{1,0:T(8,128)S(1)} collective-permute-done((f32[144,1536]{1,0:T(8,128)S(1)}, f32[144,1536]{1,0:T(8,128)S(1)}, u32[]{:S(2)}, u32[]{:S(2)}) %collective-permute-start.6) | collective-permute-done | bytes 884768 | tf_op jit(solution)/shard_map/ppermute | solution.py:15
  155.9 1.8 %maximum_add_fusion = f32[384,1536]{1,0:T(8,128)} fusion(f32[384,1536]{1,0:T(8,128)S(1)} %convolution_multiply_fusion, f32[144,1536]{1,0:T(8,128)S(1)} %collective-permute-done.6, f32[192,1536]{1,0:T(8,128)S(1)} %collective-permute-done.4, f32[32,1536]{1,0:T(8,128)S(1)} %collective-permute-done.3, f32[384]{0:T(512)S(1)} %pad.3.clone), kind=kLoop, calls=%fused_computation.3 | loop fusion | flops 2359296 | bytes 6981120 | tf_op jit(solution)/shard_map/add | solution.py:55
  157.8 0.7 fusion
  (16 shorter events, 0.3 us)
Async XLA Ops:
  1.0 14.2 %collective-permute-start = (f32[32,3072]{1,0:T(8,128)S(1)}, f32[32,3072]{1,0:T(8,128)S(1)}, u32[]{:S(2)}, u32[]{:S(2)}) collective-permute-start(f32[32,3072]{1,0:T(8,128)S(1)} %slice.15), channel_id=1, source_target_pairs={{0,14},{2,8},{4,10},{6,12},{8,22},{10,16},{12,18},{14,20},{16,30},... | collective-permute-start | bytes 1179656 | tf_op jit(solution)/shard_map/ppermute | solution.py:15
  6.2 59.7 %collective-permute-start.1 = (f32[192,3072]{1,0:T(8,128)}, f32[192,3072]{1,0:T(8,128)}, u32[]{:S(2)}, u32[]{:S(2)}) collective-permute-start(f32[192,3072]{1,0:T(8,128)} %slice.16), channel_id=1, source_target_pairs={{0,14},{2,8},{4,10},{6,12},{8,22},{10,16},{12,18},{14,20},{16,30},... | collective-permute-start | bytes 7077896 | tf_op jit(solution)/shard_map/ppermute | solution.py:15
  10.1 93.8 %collective-permute-start.2 = (f32[144,3072]{1,0:T(8,128)}, f32[144,3072]{1,0:T(8,128)}, u32[]{:S(2)}, u32[]{:S(2)}) collective-permute-start(f32[144,3072]{1,0:T(8,128)} %slice.17), channel_id=1, source_target_pairs={{0,14},{2,8},{4,10},{6,12},{8,22},{10,16},{12,18},{14,20},{16,30},... | collective-permute-start | bytes 5308424 | tf_op jit(solution)/shard_map/ppermute | solution.py:15
  13.6 93.1 %collective-permute-start.5 = (f32[16,3072]{1,0:T(8,128)}, f32[16,3072]{1,0:T(8,128)}, u32[]{:S(2)}, u32[]{:S(2)}) collective-permute-start(f32[16,3072]{1,0:T(8,128)} %slice.18), channel_id=1, source_target_pairs={{0,14},{2,8},{4,10},{6,12},{8,22},{10,16},{12,18},{14,20},{16,30},... | collective-permute-start | bytes 589832 | tf_op jit(solution)/shard_map/ppermute | solution.py:15
  15.2 50.7 %slice-start = ((s8[18874368]{0:T(1024)(128)(4,1)}), s8[4194304]{0:T(1024)(128)(4,1)S(1)}, s32[]{:S(2)}) async-start(s8[18874368]{0:T(1024)(128)(4,1)} %bitcast.11), calls=%async_computation | async-start | bytes 8388608
  15.3 50.7 %slice-start.1 = ((s8[18874368]{0:T(1024)(128)(4,1)}), s8[4194304]{0:T(1024)(128)(4,1)S(1)}, s32[]{:S(2)}) async-start(s8[18874368]{0:T(1024)(128)(4,1)} %bitcast.11), calls=%async_computation.1 | async-start | bytes 8388608
  15.3 50.7 %slice-start.2 = ((s8[18874368]{0:T(1024)(128)(4,1)}), s8[2097152]{0:T(1024)(128)(4,1)S(1)}, s32[]{:S(2)}) async-start(s8[18874368]{0:T(1024)(128)(4,1)} %bitcast.11), calls=%async_computation.2 | async-start | bytes 4194304
  25.5 40.4 %slice-start.3 = ((s8[18874368]{0:T(1024)(128)(4,1)}), s8[4194304]{0:T(1024)(128)(4,1)S(1)}, s32[]{:S(2)}) async-start(s8[18874368]{0:T(1024)(128)(4,1)} %bitcast.11), calls=%async_computation.3 | async-start | bytes 8388608
  25.5 40.5 %slice-start.4 = ((s8[18874368]{0:T(1024)(128)(4,1)}), s8[4194304]{0:T(1024)(128)(4,1)S(1)}, s32[]{:S(2)}) async-start(s8[18874368]{0:T(1024)(128)(4,1)} %bitcast.11), calls=%async_computation.4 | async-start | bytes 8388608
  103.8 7.8 %collective-permute-start.3 = (f32[32,1536]{1,0:T(8,128)}, f32[32,1536]{1,0:T(8,128)S(1)}, u32[]{:S(2)}, u32[]{:S(2)}) collective-permute-start(f32[32,1536]{1,0:T(8,128)} %convolution_multiply_fusion.3), channel_id=1, source_target_pairs={{0,24},{2,26},{4,28},{6,30},{8,0},{10,2},{12,4},{14,6},{16,8},{18,... | collective-permute-start | bytes 589832 | tf_op jit(solution)/shard_map/ppermute | solution.py:15
  105.3 50.6 %collective-permute-start.4 = (f32[192,1536]{1,0:T(8,128)S(1)}, f32[192,1536]{1,0:T(8,128)S(1)}, u32[]{:S(2)}, u32[]{:S(2)}) collective-permute-start(f32[192,1536]{1,0:T(8,128)S(1)} %convolution_multiply_fusion.1), channel_id=1, source_target_pairs={{0,24},{2,26},{4,28},{6,30},{8,0},{10,2},{12,4},{14,6},{16,8},{18,... | collective-permute-start | bytes 3538952 | tf_op jit(solution)/shard_map/ppermute | solution.py:15
  121.6 34.2 %collective-permute-start.6 = (f32[144,1536]{1,0:T(8,128)S(1)}, f32[144,1536]{1,0:T(8,128)S(1)}, u32[]{:S(2)}, u32[]{:S(2)}) collective-permute-start(f32[144,1536]{1,0:T(8,128)S(1)} %convolution_multiply_fusion.2), channel_id=1, source_target_pairs={{0,24},{2,26},{4,28},{6,30},{8,0},{10,2},{12,4},{14,6},{16,8},{18,... | collective-permute-start | bytes 2654216 | tf_op jit(solution)/shard_map/ppermute | solution.py:15
  133.1 24.7 %collective-permute-start.7 = (f32[16,1536]{1,0:T(8,128)S(1)}, f32[16,1536]{1,0:T(8,128)S(1)}, u32[]{:S(2)}, u32[]{:S(2)}) collective-permute-start(f32[16,1536]{1,0:T(8,128)S(1)} %convolution_multiply_fusion.4), channel_id=1, source_target_pairs={{0,24},{2,26},{4,28},{6,30},{8,0},{10,2},{12,4},{14,6},{16,8},{18,... | collective-permute-start | bytes 294920 | tf_op jit(solution)/shard_map/ppermute | solution.py:15

commit v6 on v5

--- a/solution.py
+++ b/solution.py
@@ -4,7 +4,7 @@
 from jax.sharding import PartitionSpec as P
 
 
-CUTS = (0, 4, 28, 46, 48)
+CUTS = (0, 3, 27, 46, 48)
 
 
 def shifted(block, rows_by, cols_by):

time: 159 us -> 159 us (level)
  transfers between devices with their start and end apart: 8 -> 8, of which waited for: 7 -> 6; matrix products, arithmetic and copies ran while one was open for 41% -> 41% of each run, Pallas kernels for 0% -> 0%
where the time goes in v6:
time: 159 us; the launch traced here: 158 us
  waiting for transfers between devices  81.1 us (51%)
  matrix products  54.7 us (34%)
  starting transfers between devices  10.3 us (6%)
  local copies, waits for them, and re-layouts  8.93 us (6%)
  other arithmetic  2.45 us (2%)
    ppermute x8, waiting for transfers between devices, shifted(): return lax.ppermute(block, ('row', 'col'), route)  81.1 us
    dot_general x5, matrix products, product(): jnp.dot(lhs_block, rhs_block, preferred_element_type=jnp.float32, precisi...  54.7 us
    ppermute x8, starting transfers between devices, shifted(): return lax.ppermute(block, ('row', 'col'), route)  10.3 us
    slice x4, local copies, waits for them, and re-layouts, body(): piece, block = lax.optimization_barrier((block[start:end], block))  8.82 us
  transfers between devices with their start and end apart: 8, of which 6 were waited for; matrix products, arithmetic and copies ran while one was open for 41% of the time, Pallas kernels for 0%

profile of v6, /device:TPU:3, one launch (start us, length us, event | category | flops | bytes accessed | tf_op | source)
XLA Modules:
  0.0 158.3 jit_solution(15532720420852366672)
XLA Ops:
  0.0 1.0 slice.15
  1.0 1.9 %collective-permute-start = (f32[24,3072]{1,0:T(8,128)S(1)}, f32[24,3072]{1,0:T(8,128)S(1)}, u32[]{:S(2)}, u32[]{:S(2)}) collective-permute-start(f32[24,3072]{1,0:T(8,128)S(1)} %slice.15), channel_id=1, source_target_pairs={{0,14},{2,8},{4,10},{6,12},{8,22},{10,16},{12,18},{14,20},{16,30},... | collective-permute-start | bytes 884744 | tf_op jit(solution)/shard_map/ppermute | solution.py:15
  2.9 3.3 %slice.16 = f32[192,3072]{1,0:T(8,128)} slice(f32[384,3072]{1,0:T(8,128)} %param.3), slice={[24:216], [0:3072]} | slice | bytes 4718592 | tf_op jit(solution)/shard_map/slice | solution.py:33
  6.2 1.0 collective-permute-start.1
  7.2 2.9 %slice.17 = f32[152,3072]{1,0:T(8,128)} slice(f32[384,3072]{1,0:T(8,128)} %param.3), slice={[216:368], [0:3072]} | slice | bytes 3735552 | tf_op jit(solution)/shard_map/slice | solution.py:33
  10.1 1.9 %collective-permute-start.2 = (f32[152,3072]{1,0:T(8,128)}, f32[152,3072]{1,0:T(8,128)}, u32[]{:S(2)}, u32[]{:S(2)}) collective-permute-start(f32[152,3072]{1,0:T(8,128)} %slice.17), channel_id=1, source_target_pairs={{0,14},{2,8},{4,10},{6,12},{8,22},{10,16},{12,18},{14,20},{16,30},... | collective-permute-start | bytes 5603336 | tf_op jit(solution)/shard_map/ppermute | solution.py:15
  12.0 1.6 %slice.18 = f32[16,3072]{1,0:T(8,128)} slice(f32[384,3072]{1,0:T(8,128)} %param.3), slice={[368:384], [0:3072]} | slice | bytes 393216 | tf_op jit(solution)/shard_map/slice | solution.py:33
  13.6 0.6 collective-permute-start.5
  14.9 8.9 %convolution_multiply_fusion.3 = f32[24,1536]{1,0:T(8,128)S(1)} fusion(f32[24,3072]{1,0:T(8,128)S(1)} %collective-permute-done, f32[3072,1536]{1,0:T(8,128)} %param.4, f32[]{:T(128)} %bitcast), kind=kOutput, calls=%fused_computation.4 | convolution fusion | flops 679514112 | bytes 19316740 | tf_op jit(solution)/shard_map/dot_general | solution.py:23
  23.8 17.0 %convolution_multiply_fusion = f32[384,1536]{1,0:T(8,128)S(1)} fusion(f32[384,3072]{1,0:T(8,128)} %param.3, f32[3072,1536]{1,0:T(8,128)} %param.4, f32[]{:T(128)} %bitcast), kind=kOutput, calls=%fused_computation | convolution fusion | flops 10872225792 | bytes 25952260 | tf_op jit(solution)/shard_map/dot_general | solution.py:23
  40.8 21.9 %collective-permute-done.1 = f32[192,3072]{1,0:T(8,128)} collective-permute-done((f32[192,3072]{1,0:T(8,128)}, f32[192,3072]{1,0:T(8,128)}, u32[]{:S(2)}, u32[]{:S(2)}) %collective-permute-start.1) | collective-permute-done | bytes 2359328 | tf_op jit(solution)/shard_map/ppermute | solution.py:15
  62.8 9.7 %convolution_multiply_fusion.1 = f32[192,1536]{1,0:T(8,128)S(1)} fusion(f32[192,3072]{1,0:T(8,128)} %collective-permute-done.1, f32[3072,1536]{1,0:T(8,128)S(1)} %bitcast.12, f32[]{:T(128)} %bitcast), kind=kOutput, calls=%fused_computation.1 | convolution fusion | flops 5436112896 | bytes 22413316 | tf_op jit(solution)/shard_map/dot_general | solution.py:23
  72.4 30.3 %collective-permute-done.2 = f32[152,3072]{1,0:T(8,128)} collective-permute-done((f32[152,3072]{1,0:T(8,128)}, f32[152,3072]{1,0:T(8,128)}, u32[]{:S(2)}, u32[]{:S(2)}) %collective-permute-start.2) | collective-permute-done | bytes 1867808 | tf_op jit(solution)/shard_map/ppermute | solution.py:15
  102.8 2.5 %collective-permute-start.3 = (f32[24,1536]{1,0:T(8,128)S(1)}, f32[24,1536]{1,0:T(8,128)S(1)}, u32[]{:S(2)}, u32[]{:S(2)}) collective-permute-start(f32[24,1536]{1,0:T(8,128)S(1)} %convolution_multiply_fusion.3), channel_id=1, source_target_pairs={{0,24},{2,26},{4,28},{6,30},{8,0},{10,2},{12,4},{14,6},{16,8},{18,... | collective-permute-start | bytes 442376 | tf_op jit(solution)/shard_map/ppermute | solution.py:15
  105.3 1.3 collective-permute-done.5
  106.6 3.7 %collective-permute-done.3 = f32[24,1536]{1,0:T(8,128)S(1)} collective-permute-done((f32[24,1536]{1,0:T(8,128)S(1)}, f32[24,1536]{1,0:T(8,128)S(1)}, u32[]{:S(2)}, u32[]{:S(2)}) %collective-permute-start.3) | collective-permute-done | bytes 147488 | tf_op jit(solution)/shard_map/ppermute | solution.py:15
  110.3 10.2 %convolution_multiply_fusion.2 = f32[152,1536]{1,0:T(8,128)S(1)} fusion(f32[152,3072]{1,0:T(8,128)} %collective-permute-done.2, f32[3072,1536]{1,0:T(8,128)} %param.4, f32[]{:T(128)} %bitcast), kind=kOutput, calls=%fused_computation.2 | convolution fusion | flops 4303589376 | bytes 21676036 | tf_op jit(solution)/shard_map/dot_general | solution.py:23
  120.5 2.4 %collective-permute-start.6 = (f32[152,1536]{1,0:T(8,128)S(1)}, f32[152,1536]{1,0:T(8,128)S(1)}, u32[]{:S(2)}, u32[]{:S(2)}) collective-permute-start(f32[152,1536]{1,0:T(8,128)S(1)} %convolution_multiply_fusion.2), channel_id=1, source_target_pairs={{0,24},{2,26},{4,28},{6,30},{8,0},{10,2},{12,4},{14,6},{16,8},{18,... | collective-permute-start | bytes 2801672 | tf_op jit(solution)/shard_map/ppermute | solution.py:15
  122.9 0.1 pad.3.clone
  123.0 9.0 %convolution_multiply_fusion.4 = f32[16,1536]{1,0:T(8,128)S(1)} fusion(f32[16,3072]{1,0:T(8,128)} %collective-permute-done.5, f32[3072,1536]{1,0:T(8,128)} %param.4, f32[]{:T(128)} %bitcast), kind=kOutput, calls=%fused_computation.5 | convolution fusion | flops 453009408 | bytes 19169284 | tf_op jit(solution)/shard_map/dot_general | solution.py:23
  132.0 23.6 %collective-permute-done.6 = f32[152,1536]{1,0:T(8,128)S(1)} collective-permute-done((f32[152,1536]{1,0:T(8,128)S(1)}, f32[152,1536]{1,0:T(8,128)S(1)}, u32[]{:S(2)}, u32[]{:S(2)}) %collective-permute-start.6) | collective-permute-done | bytes 933920 | tf_op jit(solution)/shard_map/ppermute | solution.py:15
  155.6 1.8 %maximum_add_fusion = f32[384,1536]{1,0:T(8,128)} fusion(f32[384,1536]{1,0:T(8,128)S(1)} %convolution_multiply_fusion, f32[152,1536]{1,0:T(8,128)S(1)} %collective-permute-done.6, f32[192,1536]{1,0:T(8,128)S(1)} %collective-permute-done.4, f32[24,1536]{1,0:T(8,128)S(1)} %collective-permute-done.3, f32[384]{0:T(512)S(1)} %pad.3.clone), kind=kLoop, calls=%fused_computation.3 | loop fusion | flops 2359296 | bytes 6981120 | tf_op jit(solution)/shard_map/add | solution.py:55
  157.4 0.3 collective-permute-done.7
  157.7 0.7 fusion
  (16 shorter events, 0.1 us)
Async XLA Ops:
  1.0 13.8 %collective-permute-start = (f32[24,3072]{1,0:T(8,128)S(1)}, f32[24,3072]{1,0:T(8,128)S(1)}, u32[]{:S(2)}, u32[]{:S(2)}) collective-permute-start(f32[24,3072]{1,0:T(8,128)S(1)} %slice.15), channel_id=1, source_target_pairs={{0,14},{2,8},{4,10},{6,12},{8,22},{10,16},{12,18},{14,20},{16,30},... | collective-permute-start | bytes 884744 | tf_op jit(solution)/shard_map/ppermute | solution.py:15
  6.2 56.5 %collective-permute-start.1 = (f32[192,3072]{1,0:T(8,128)}, f32[192,3072]{1,0:T(8,128)}, u32[]{:S(2)}, u32[]{:S(2)}) collective-permute-start(f32[192,3072]{1,0:T(8,128)} %slice.16), channel_id=1, source_target_pairs={{0,14},{2,8},{4,10},{6,12},{8,22},{10,16},{12,18},{14,20},{16,30},... | collective-permute-start | bytes 7077896 | tf_op jit(solution)/shard_map/ppermute | solution.py:15
  10.1 92.6 %collective-permute-start.2 = (f32[152,3072]{1,0:T(8,128)}, f32[152,3072]{1,0:T(8,128)}, u32[]{:S(2)}, u32[]{:S(2)}) collective-permute-start(f32[152,3072]{1,0:T(8,128)} %slice.17), channel_id=1, source_target_pairs={{0,14},{2,8},{4,10},{6,12},{8,22},{10,16},{12,18},{14,20},{16,30},... | collective-permute-start | bytes 5603336 | tf_op jit(solution)/shard_map/ppermute | solution.py:15
  13.6 93.0 %collective-permute-start.5 = (f32[16,3072]{1,0:T(8,128)}, f32[16,3072]{1,0:T(8,128)}, u32[]{:S(2)}, u32[]{:S(2)}) collective-permute-start(f32[16,3072]{1,0:T(8,128)} %slice.18), channel_id=1, source_target_pairs={{0,14},{2,8},{4,10},{6,12},{8,22},{10,16},{12,18},{14,20},{16,30},... | collective-permute-start | bytes 589832 | tf_op jit(solution)/shard_map/ppermute | solution.py:15
  14.8 47.9 %slice-start = ((s8[18874368]{0:T(1024)(128)(4,1)}), s8[4194304]{0:T(1024)(128)(4,1)S(1)}, s32[]{:S(2)}) async-start(s8[18874368]{0:T(1024)(128)(4,1)} %bitcast.11), calls=%async_computation | async-start | bytes 8388608
  14.8 47.9 %slice-start.1 = ((s8[18874368]{0:T(1024)(128)(4,1)}), s8[4194304]{0:T(1024)(128)(4,1)S(1)}, s32[]{:S(2)}) async-start(s8[18874368]{0:T(1024)(128)(4,1)} %bitcast.11), calls=%async_computation.1 | async-start | bytes 8388608
  14.9 47.9 %slice-start.2 = ((s8[18874368]{0:T(1024)(128)(4,1)}), s8[2097152]{0:T(1024)(128)(4,1)S(1)}, s32[]{:S(2)}) async-start(s8[18874368]{0:T(1024)(128)(4,1)} %bitcast.11), calls=%async_computation.2 | async-start | bytes 4194304
  23.8 38.9 %slice-start.3 = ((s8[18874368]{0:T(1024)(128)(4,1)}), s8[4194304]{0:T(1024)(128)(4,1)S(1)}, s32[]{:S(2)}) async-start(s8[18874368]{0:T(1024)(128)(4,1)} %bitcast.11), calls=%async_computation.3 | async-start | bytes 8388608
  23.8 38.9 %slice-start.4 = ((s8[18874368]{0:T(1024)(128)(4,1)}), s8[4194304]{0:T(1024)(128)(4,1)S(1)}, s32[]{:S(2)}) async-start(s8[18874368]{0:T(1024)(128)(4,1)} %bitcast.11), calls=%async_computation.4 | async-start | bytes 8388608
  102.8 7.5 %collective-permute-start.3 = (f32[24,1536]{1,0:T(8,128)S(1)}, f32[24,1536]{1,0:T(8,128)S(1)}, u32[]{:S(2)}, u32[]{:S(2)}) collective-permute-start(f32[24,1536]{1,0:T(8,128)S(1)} %convolution_multiply_fusion.3), channel_id=1, source_target_pairs={{0,24},{2,26},{4,28},{6,30},{8,0},{10,2},{12,4},{14,6},{16,8},{18,... | collective-permute-start | bytes 442376 | tf_op jit(solution)/shard_map/ppermute | solution.py:15
  105.2 50.3 %collective-permute-start.4 = (f32[192,1536]{1,0:T(8,128)S(1)}, f32[192,1536]{1,0:T(8,128)S(1)}, u32[]{:S(2)}, u32[]{:S(2)}) collective-permute-start(f32[192,1536]{1,0:T(8,128)S(1)} %convolution_multiply_fusion.1), channel_id=1, source_target_pairs={{0,24},{2,26},{4,28},{6,30},{8,0},{10,2},{12,4},{14,6},{16,8},{18,... | collective-permute-start | bytes 3538952 | tf_op jit(solution)/shard_map/ppermute | solution.py:15
  120.5 35.1 %collective-permute-start.6 = (f32[152,1536]{1,0:T(8,128)S(1)}, f32[152,1536]{1,0:T(8,128)S(1)}, u32[]{:S(2)}, u32[]{:S(2)}) collective-permute-start(f32[152,1536]{1,0:T(8,128)S(1)} %convolution_multiply_fusion.2), channel_id=1, source_target_pairs={{0,24},{2,26},{4,28},{6,30},{8,0},{10,2},{12,4},{14,6},{16,8},{18,... | collective-permute-start | bytes 2801672 | tf_op jit(solution)/shard_map/ppermute | solution.py:15
  131.9 25.7 %collective-permute-start.7 = (f32[16,1536]{1,0:T(8,128)S(1)}, f32[16,1536]{1,0:T(8,128)S(1)}, u32[]{:S(2)}, u32[]{:S(2)}) collective-permute-start(f32[16,1536]{1,0:T(8,128)S(1)} %convolution_multiply_fusion.4), channel_id=1, source_target_pairs={{0,24},{2,26},{4,28},{6,30},{8,0},{10,2},{12,4},{14,6},{16,8},{18,... | collective-permute-start | bytes 294920 | tf_op jit(solution)/shard_map/ppermute | solution.py:15
